TPU v7x, 32 devices: a whole 2x2x4 slice. The times are simulated.
32 devices in a mesh: dp: 4 (over z), seq: 2 (over y), head: 4 (over x, core).
Axes of the slice: x: 2, y: 2, z: 4, core: 2. Of those that a mesh axis runs over, the one named last changes fastest.
Arguments:
- frames: bfloat16 [4, 1536, 768], P('dp', 'seq'), may hold values from -6 to 6
- lengths: int32 [4], P('dp'), may hold values from 1152 to 1536, as said below
- grad_out: bfloat16 [4, 1536, 768], P('dp', 'seq'), may hold values from -6 to 6
- w_qkv: bfloat16 [2, 3, 768, 768], P(None, None, 'seq', 'head'), may hold values from -0.21875 to 0.21875
- qv_bias: bfloat16 [2, 2, 768], P(None, None, 'head'), may hold values from -0.75 to 0.75
- w_out: bfloat16 [2, 768, 768], P(None, 'head', 'seq'), may hold values from -6 to 6
- w_up: bfloat16 [2, 768, 3072], P(None, 'seq', 'head'), may hold values from -0.21875 to 0.21875
- up_bias: bfloat16 [2, 3072], P(None, 'head'), may hold values from -4 to 4
- w_down: bfloat16 [2, 3072, 768], P(None, 'head', 'seq'), may hold values from -0.109375 to 0.109375
- gains: bfloat16 [2, 2, 768], P(None, None, 'seq'), may hold values from 0.25 to 1.75
- shifts: bfloat16 [2, 4, 768], P(None, None, 'seq'), may hold values from -4 to 4
Outputs:
- out: bfloat16 [4, 1536, 768], P('dp', 'seq')
- grad_frames: float32 [4, 1536, 768], P('dp', 'seq')
- grad_w_qkv: float32 [2, 3, 768, 768], P(None, None, 'seq', 'head')
- grad_qv_bias: float32 [2, 2, 768], P(None, None, 'head')
- grad_w_out: float32 [2, 768, 768], P(None, 'head', 'seq')
- grad_w_up: float32 [2, 768, 3072], P(None, 'seq', 'head')
- grad_up_bias: float32 [2, 3072], P(None, 'head')
- grad_w_down: float32 [2, 3072, 768], P(None, 'head', 'seq')
- grad_gains: float32 [2, 2, 768], P(None, None, 'seq')
- grad_shifts: float32 [2, 4, 768], P(None, None, 'seq')
Inputs may be any that keep to these rules, and one draw needn't show every extreme that they name: `lengths`: each clip's number of valid frames; keys at or past it are masked; some clip has all 1536 frames valid.
All inputs are finite; a program needn't handle non-finite values.
Results may differ from a plain program's by a relative error of at most 0.018.
Values may be sent and summed in bfloat16 or wider, within the bound.
A program may use at most 192 MiB of HBM per device.

v0:
```python
import jax
import jax.numpy as jnp
from jax import lax
from jax.sharding import PartitionSpec as P

HD = 64


epsilon = 1e-05


def normalize(values, gain_vector, shift_vector):
    row_mean = jnp.mean(values, axis=-1, keepdims=True)
    centered = values - row_mean
    variance = jnp.mean(centered * centered, axis=-1, keepdims=True)
    return centered * lax.rsqrt(variance + epsilon) * gain_vector + shift_vector


def gelu_exact(values):
    return jax.nn.gelu(values, approximate=False)


def column_sum(values):
    return jnp.sum(values.astype(jnp.float32), axis=0)


def stack_member(collected, position):
    return jnp.stack([entry[position] for entry in collected])


def to_heads(values, head_count):
    clip_count, row_total, head_width = values.shape
    return values.reshape(clip_count, row_total, head_count, HD).transpose(0, 2, 1, 3)


def from_heads(values):
    clip_count, head_count, row_total, head_size = values.shape
    return values.transpose(0, 2, 1, 3).reshape(clip_count, row_total, head_count * head_size)


def attend(queries, key_all, value_all, key_valid, head_count):
    clip_count, rows_dev, head_width = queries.shape
    scores = jnp.einsum(
        "chqe,chke->chqk",
        to_heads(queries, head_count),
        to_heads(key_all, head_count),
        preferred_element_type=jnp.float32,
    )
    scores = jnp.where(key_valid[:, None, None, :], scores, -1e30)
    row_peak = jnp.max(scores, axis=-1, keepdims=True)
    powered = jnp.exp(scores - row_peak)
    row_total = jnp.sum(powered, axis=-1, keepdims=True)
    probs_low = (powered / row_total).astype(jnp.bfloat16)
    attended = jnp.einsum(
        "chqk,chke->chqe",
        probs_low,
        to_heads(value_all, head_count),
        preferred_element_type=jnp.float32,
    )
    attended = from_heads(attended).reshape(clip_count * rows_dev, head_width).astype(jnp.bfloat16)
    return (attended, row_peak + jnp.log(row_total))


def attend_back(queries, key_all, value_all, key_valid, logsum, d_attended, head_count):
    clip_count, rows_dev, head_width = queries.shape
    query_heads = to_heads(queries, head_count)
    key_heads = to_heads(key_all, head_count)
    value_heads = to_heads(value_all, head_count)
    grad_heads = to_heads(d_attended.reshape(clip_count, rows_dev, head_width), head_count)
    scores = jnp.einsum(
        "chqe,chke->chqk", query_heads, key_heads, preferred_element_type=jnp.float32
    )
    scores = jnp.where(key_valid[:, None, None, :], scores, -1e30)
    probs = jnp.exp(scores - logsum)
    probs_low = probs.astype(jnp.bfloat16)
    d_value = jnp.einsum(
        "chqk,chqe->chke", probs_low, grad_heads, preferred_element_type=jnp.float32
    )
    d_probs = jnp.einsum(
        "chqe,chke->chqk", grad_heads, value_heads, preferred_element_type=jnp.float32
    )
    row_inner = jnp.sum(probs * d_probs, axis=-1, keepdims=True)
    d_scores = (probs * (d_probs - row_inner)).astype(jnp.bfloat16)
    d_query = jnp.einsum("chqk,chke->chqe", d_scores, key_heads, preferred_element_type=jnp.float32)
    d_key = jnp.einsum("chqk,chqe->chke", d_scores, query_heads, preferred_element_type=jnp.float32)
    return (
        from_heads(d_query).reshape(clip_count * rows_dev, head_width),
        from_heads(d_key),
        from_heads(d_value),
    )


def on_device(
    frames, lengths, grad_out, w_qkv, qv_bias, w_out, w_up, up_bias, w_down, gains, shifts
):
    clip_count, rows_dev, model_width = frames.shape
    row_count = clip_count * rows_dev
    layers = w_qkv.shape[0]
    head_width = w_qkv.shape[3]
    head_count = head_width // HD
    query_scale = HD ** (-0.5)
    key_length = rows_dev * lax.axis_size("seq")
    positions = jnp.arange(key_length, dtype=jnp.int32)
    key_valid = positions[None, :] < lengths[:, None]
    stream = frames.astype(jnp.float32).reshape(row_count, model_width)
    saved_layers = []
    for layer_index in range(layers):
        weight_full = (
            lax.all_gather(w_qkv[layer_index], "seq", axis=1, tiled=True),
            lax.all_gather(w_out[layer_index], "seq", axis=1, tiled=True),
            lax.all_gather(w_up[layer_index], "seq", axis=0, tiled=True),
            lax.all_gather(w_down[layer_index], "seq", axis=1, tiled=True),
            lax.all_gather(gains[layer_index], "seq", axis=1, tiled=True),
            lax.all_gather(shifts[layer_index], "seq", axis=1, tiled=True),
        )
        qkv_full, out_full, up_full, down_full, gain_full, shift_full = weight_full
        gain_pair = gain_full.astype(jnp.float32)
        shift_set = shift_full.astype(jnp.float32)
        bias_pair = qv_bias[layer_index].astype(jnp.float32)
        normed = normalize(stream, gain_pair[0], shift_set[0]).astype(jnp.bfloat16)
        projected = jnp.einsum("rd,kdc->krc", normed, qkv_full, preferred_element_type=jnp.float32)
        queries = ((projected[0] + bias_pair[0]) * query_scale).astype(jnp.bfloat16)
        queries = queries.reshape(clip_count, rows_dev, head_width)
        key_rows = projected[1].astype(jnp.bfloat16).reshape(clip_count, rows_dev, head_width)
        value_rows = (
            (projected[2] + bias_pair[1])
            .astype(jnp.bfloat16)
            .reshape(clip_count, rows_dev, head_width)
        )
        key_all, value_all = (
            lax.all_gather(key_rows, "seq", axis=1, tiled=True),
            lax.all_gather(value_rows, "seq", axis=1, tiled=True),
        )
        attended, logsum = attend(queries, key_all, value_all, key_valid, head_count)
        attn_part = jnp.dot(attended, out_full, preferred_element_type=jnp.float32)
        mid = stream + lax.psum(attn_part, "head") + shift_set[1]
        normed_two = normalize(mid, gain_pair[1], shift_set[2]).astype(jnp.bfloat16)
        hidden_pre = jnp.dot(normed_two, up_full, preferred_element_type=jnp.float32) + up_bias[
            layer_index
        ].astype(jnp.float32)
        activated = gelu_exact(hidden_pre).astype(jnp.bfloat16)
        down_part = jnp.dot(activated, down_full, preferred_element_type=jnp.float32)
        saved_layers.append(
            (
                stream,
                mid,
                normed,
                queries,
                key_rows,
                value_rows,
                key_all,
                value_all,
                logsum,
                attended,
                normed_two,
                hidden_pre,
                weight_full,
            )
        )
        stream = (
            mid
            + lax.psum(down_part.astype(jnp.bfloat16), "head").astype(jnp.float32)
            + shift_set[3]
        )
    output = stream.astype(jnp.bfloat16).reshape(clip_count, rows_dev, model_width)
    grad_stream = grad_out.astype(jnp.float32).reshape(row_count, model_width)
    owned_grads = [None] * layers
    bias_grads = [None] * layers
    for layer_index in range(layers - 1, -1, -1):
        (
            stream_in,
            mid,
            normed,
            queries,
            key_rows,
            value_rows,
            key_all,
            value_all,
            logsum,
            attended,
            normed_two,
            hidden_pre,
            weight_full,
        ) = saved_layers[layer_index]
        weight_full = (
            lax.all_gather(w_qkv[layer_index], "seq", axis=1, tiled=True),
            lax.all_gather(w_out[layer_index], "seq", axis=1, tiled=True),
            lax.all_gather(w_up[layer_index], "seq", axis=0, tiled=True),
            lax.all_gather(w_down[layer_index], "seq", axis=1, tiled=True),
            lax.all_gather(gains[layer_index], "seq", axis=1, tiled=True),
            lax.all_gather(shifts[layer_index], "seq", axis=1, tiled=True),
        )
        key_all, value_all = (
            lax.all_gather(key_rows, "seq", axis=1, tiled=True),
            lax.all_gather(value_rows, "seq", axis=1, tiled=True),
        )
        qkv_full, out_full, up_full, down_full, gain_full, shift_full = weight_full
        gain_pair = gain_full.astype(jnp.float32)
        shift_set = shift_full.astype(jnp.float32)
        grad_low = grad_stream.astype(jnp.bfloat16)
        activated = gelu_exact(hidden_pre).astype(jnp.bfloat16)
        d_shift_mlp = column_sum(grad_low)
        d_down = jnp.dot(activated.T, grad_low, preferred_element_type=jnp.float32)
        d_act = jnp.dot(grad_low, down_full.T, preferred_element_type=jnp.float32)
        gelu_value, gelu_pull = jax.vjp(gelu_exact, hidden_pre)
        d_hidden = gelu_pull(d_act)[0].astype(jnp.bfloat16)
        d_up = jnp.dot(normed_two.T, d_hidden, preferred_element_type=jnp.float32)
        d_up_bias = column_sum(d_hidden)
        d_norm_two = lax.psum(
            jnp.dot(d_hidden, up_full.T, preferred_element_type=jnp.float32).astype(jnp.bfloat16),
            "head",
        ).astype(jnp.float32)
        norm_value, norm_pull = jax.vjp(normalize, mid, gain_pair[1], shift_set[2])
        d_mid, d_gain_two, d_shift_two = norm_pull(d_norm_two)
        grad_stream = grad_stream + d_mid
        grad_low = grad_stream.astype(jnp.bfloat16)
        d_shift_attn = column_sum(grad_low)
        d_out = jnp.dot(attended.T, grad_low, preferred_element_type=jnp.float32)
        d_attended = jnp.dot(grad_low, out_full.T, preferred_element_type=jnp.float32).astype(
            jnp.bfloat16
        )
        d_query, d_key_part, d_value_part = attend_back(
            queries, key_all, value_all, key_valid, logsum, d_attended, head_count
        )
        d_key, d_value = (
            lax.psum_scatter(
                d_key_part.astype(jnp.bfloat16), "seq", scatter_dimension=1, tiled=True
            ).astype(jnp.float32),
            lax.psum_scatter(
                d_value_part.astype(jnp.bfloat16), "seq", scatter_dimension=1, tiled=True
            ).astype(jnp.float32),
        )
        d_query_pre = d_query.astype(jnp.bfloat16) * jnp.asarray(query_scale, jnp.bfloat16)
        d_key_low = d_key.astype(jnp.bfloat16).reshape(row_count, head_width)
        d_value_low = d_value.astype(jnp.bfloat16).reshape(row_count, head_width)
        d_qkv = jnp.stack([d_query_pre, d_key_low, d_value_low], axis=0)
        d_qkv_weight = jnp.einsum("rd,krc->kdc", normed, d_qkv, preferred_element_type=jnp.float32)
        d_bias_pair = jnp.stack([column_sum(d_query_pre), column_sum(d_value_low)])
        d_normed_part = jnp.einsum(
            "krc,kdc->rd", d_qkv, qkv_full, preferred_element_type=jnp.float32
        )
        d_normed = lax.psum(d_normed_part.astype(jnp.bfloat16), "head").astype(jnp.float32)
        norm_value, norm_pull = jax.vjp(normalize, stream_in, gain_pair[0], shift_set[0])
        d_before, d_gain_one, d_shift_one = norm_pull(d_normed)
        grad_stream = grad_stream + d_before
        d_gains = jnp.stack([d_gain_one, d_gain_two])
        d_shifts = jnp.stack([d_shift_one, d_shift_attn, d_shift_two, d_shift_mlp])
        share_qkv, share_out, share_up, share_down, share_gains, share_shifts = (
            lax.psum_scatter(
                d_qkv_weight.astype(jnp.bfloat16), "seq", scatter_dimension=1, tiled=True
            ).astype(jnp.float32),
            lax.psum_scatter(
                d_out.astype(jnp.bfloat16), "seq", scatter_dimension=1, tiled=True
            ).astype(jnp.float32),
            lax.psum_scatter(
                d_up.astype(jnp.bfloat16), "seq", scatter_dimension=0, tiled=True
            ).astype(jnp.float32),
            lax.psum_scatter(
                d_down.astype(jnp.bfloat16), "seq", scatter_dimension=1, tiled=True
            ).astype(jnp.float32),
            lax.psum_scatter(
                d_gains.astype(jnp.bfloat16), "seq", scatter_dimension=1, tiled=True
            ).astype(jnp.float32),
            lax.psum_scatter(
                d_shifts.astype(jnp.bfloat16), "seq", scatter_dimension=1, tiled=True
            ).astype(jnp.float32),
        )
        share_qkv, share_out, share_up, share_down, share_gains, share_shifts = (
            lax.psum(share_qkv.astype(jnp.bfloat16), "dp").astype(jnp.float32),
            lax.psum(share_out.astype(jnp.bfloat16), "dp").astype(jnp.float32),
            lax.psum(share_up.astype(jnp.bfloat16), "dp").astype(jnp.float32),
            lax.psum(share_down.astype(jnp.bfloat16), "dp").astype(jnp.float32),
            lax.psum(share_gains.astype(jnp.bfloat16), "dp").astype(jnp.float32),
            lax.psum(share_shifts.astype(jnp.bfloat16), "dp").astype(jnp.float32),
        )
        owned_grads[layer_index] = (
            share_qkv,
            share_out,
            share_up,
            share_down,
            share_gains,
            share_shifts,
        )
        bias_grads[layer_index] = (d_bias_pair, d_up_bias)
    grad_qkv = stack_member(owned_grads, 0)
    grad_out_weight = stack_member(owned_grads, 1)
    grad_up_weight = stack_member(owned_grads, 2)
    grad_down_weight = stack_member(owned_grads, 3)
    grad_gain_set = stack_member(owned_grads, 4)
    grad_shift_set = stack_member(owned_grads, 5)
    grad_bias_pair, grad_bias_up = lax.psum(
        (stack_member(bias_grads, 0), stack_member(bias_grads, 1)), ("dp", "seq")
    )
    grad_frames = grad_stream.reshape(clip_count, rows_dev, model_width)
    return (
        output,
        grad_frames,
        grad_qkv,
        grad_bias_pair,
        grad_out_weight,
        grad_up_weight,
        grad_bias_up,
        grad_down_weight,
        grad_gain_set,
        grad_shift_set,
    )


def solution(mesh):
    return jax.shard_map(
        on_device,
        mesh=mesh,
        in_specs=(
            P("dp", "seq", None),
            P("dp"),
            P("dp", "seq", None),
            P(None, None, "seq", "head"),
            P(None, None, "head"),
            P(None, "head", "seq"),
            P(None, "seq", "head"),
            P(None, "head"),
            P(None, "head", "seq"),
            P(None, None, "seq"),
            P(None, None, "seq"),
        ),
        out_specs=(
            P("dp", "seq", None),
            P("dp", "seq", None),
            P(None, None, "seq", "head"),
            P(None, None, "head"),
            P(None, "head", "seq"),
            P(None, "seq", "head"),
            P(None, "head"),
            P(None, "head", "seq"),
            P(None, None, "seq"),
            P(None, None, "seq"),
        ),
        check_vma=False,
    )
```

profile of v0, /device:TPU:0, one launch (start us, length us, event | category | flops | bytes accessed | tf_op | source)
XLA Modules:
  0.0 904.3 jit_solution(18069571852587356720)
XLA Ops:
  34.2 9.4 %all-gather.2 = bf16[1,3,768,192]{2,3,1,0:T(8,128)(2,1)S(1)} all-gather(bf16[1,3,384,192]{2,3,1,0:T(8,128)(2,1)S(1)} %get-tuple-element.78), channel_id=4, replica_groups=mesh['dp'=4,'seq'=2,'head'=4] {'seq'}, dimensions={2}, use_global_device_ids=true | all-gather | bytes 1327104 | tf_op jit(solution)/shard_map/all_gather | solution.py:109
  45.6 8.7 all_gather.66
  92.7 53.8 %all-reduce.13.cloned.1.call-done = f32[768,768]{1,0:T(8,128)} async-done(((f32[768,768]{1,0:T(8,128)}), f32[768,768]{1,0:T(8,128)}) %all-reduce.13.cloned.1.call-update) | async-done | bytes 2359312 | tf_op jit(solution)/shard_map/psum | solution.py:136
  149.3 8.9 multiply_convert_fusion.3
  178.0 9.5 %all-gather.8 = bf16[1,3,768,192]{2,3,1,0:T(8,128)(2,1)} all-gather(bf16[1,3,384,192]{2,3,1,0:T(8,128)(2,1)S(1)} %copy-done.37), channel_id=10, replica_groups=mesh['dp'=4,'seq'=2,'head'=4] {'seq'}, dimensions={2}, use_global_device_ids=true | all-gather | bytes 1327104 | tf_op jit(solution)/shard_map/all_gather | solution.py:109
  187.5 12.1 %all-reduce.15.cloned.1.call-done = bf16[768,768]{1,0:T(8,128)(2,1)} async-done(((bf16[768,768]{1,0:T(8,128)(2,1)}), bf16[768,768]{1,0:T(8,128)(2,1)}) %all-reduce.15.cloned.1.call-update) | async-done | bytes 1179664 | tf_op jit(solution)/shard_map/psum | solution.py:162
  204.7 9.4 %all_gather.74 = bf16[1,1536,192]{1,2,0:T(8,128)(2,1)S(1)} all-gather(bf16[1,768,192]{1,2,0:T(8,128)(2,1)S(1)} %get-tuple-element.68), channel_id=1, replica_groups=mesh['dp'=4,'seq'=2,'head'=4] {'seq'}, dimensions={1}, use_global_device_ids=true | all-gather | bytes 884736 | tf_op jit(solution)/shard_map/all_gather | solution.py:132
  255.0 54.6 %all-reduce.17.cloned.1.call-done = f32[768,768]{1,0:T(8,128)} async-done(((f32[768,768]{1,0:T(8,128)}), f32[768,768]{1,0:T(8,128)}) %all-reduce.17.cloned.1.call-update) | async-done | bytes 2359312 | tf_op jit(solution)/shard_map/psum | solution.py:136
  314.1 9.2 %multiply_convert_fusion.2 = (bf16[768,768]{1,0:T(8,128)(2,1)}, f32[768,768]{1,0:T(8,128)}, f32[768,768]{1,0:T(8,128)}) fusion(f32[768]{0:T(1024)} %get-tuple-element.30, bf16[1,768,768]{2,1,0:T(8,128)(2,1)} %all-gather.21.cloned.1.call-done, f32[768,768]{1,0:T(8,128)} %copy-done, f32[768]{0:T(1024)} %get-tuple-element.19, f32[768]{0:T(1024)S(1)} %copy-done.84, ...), kind=kOutput, calls=%fused_computation.81 | convolution fusion | flops 947847168 | bytes 9452544 | tf_op jit(solution)/shard_map/dot_general | solution.py:138
  332.9 36.3 %all-reduce.19.cloned.1.call-done = bf16[768,768]{1,0:T(8,128)(2,1)} async-done(((bf16[768,768]{1,0:T(8,128)(2,1)}), bf16[768,768]{1,0:T(8,128)(2,1)}) %all-reduce.19.cloned.1.call-update) | async-done | bytes 1179664 | tf_op jit(solution)/shard_map/psum | solution.py:209
  395.1 10.7 %multiply_convert_fusion.1 = bf16[3,768,1536]{2,1,0:T(8,128)(2,1)S(1)} fusion(f32[3,768,1536]{2,1,0:T(8,128)} %get-tuple-element.110, f32[3,768,1536]{2,1,0:T(8,128)} %get-tuple-element.107, f32[3,768]{1,0:T(4,128)} %get-tuple-element.109, f32[3,768]{1,0:T(4,128)S(1)} %log_add_fusion.1, pred[1536]{0:T(1024)(128)(4,1)S(1)} %iota_compare_fusion), kind=kLoop, calls=%fused_computation.3 | loop fusion | flops 17694720 | bytes 35409408 | tf_op jit(solution)/shard_map/convert_element_type | solution.py:83
  415.6 12.5 %reduce-scatter.37.cloned.1.call-done = bf16[1,768,192]{1,2,0:T(8,128)(2,1)} async-done(((bf16[1,1536,192]{1,2,0:T(8,128)(2,1)}), bf16[1,768,192]{1,2,0:T(8,128)(2,1)}) %reduce-scatter.37.cloned.1.call-update) | async-done | bytes 294928 | tf_op jit(solution)/shard_map/reduce_scatter | solution.py:226
  431.9 37.2 %all-reduce.21.cloned.1.call-done = bf16[768,768]{1,0:T(8,128)(2,1)} async-done(((bf16[768,768]{1,0:T(8,128)(2,1)}), bf16[768,768]{1,0:T(8,128)(2,1)}) %all-reduce.21.cloned.1.call-update) | async-done | bytes 1179664 | tf_op jit(solution)/shard_map/psum | solution.py:242
  482.1 36.9 %all-reduce.23.cloned.1.call-done = bf16[768,768]{1,0:T(8,128)(2,1)} async-done(((bf16[768,768]{1,0:T(8,128)(2,1)}), bf16[768,768]{1,0:T(8,128)(2,1)}) %all-reduce.23.cloned.1.call-update) | async-done | bytes 1179664 | tf_op jit(solution)/shard_map/psum | solution.py:209
  540.7 10.6 %multiply_convert_fusion = bf16[3,768,1536]{2,1,0:T(8,128)(2,1)S(1)} fusion(f32[3,768,1536]{2,1,0:T(8,128)} %get-tuple-element.112, f32[3,768,1536]{2,1,0:T(8,128)} %get-tuple-element.104, f32[3,768]{1,0:T(4,128)S(1)} %get-tuple-element.111, f32[3,768]{1,0:T(4,128)S(1)} %log_add_fusion, pred[1536]{0:T(1024)(128)(4,1)S(1)} %iota_compare_fusion), kind=kLoop, calls=%fused_computation | loop fusion | flops 17694720 | bytes 35409408 | tf_op jit(solution)/shard_map/convert_element_type | solution.py:83
  561.1 12.2 %reduce-scatter.41.cloned.1.call-done = bf16[1,768,192]{1,2,0:T(8,128)(2,1)} async-done(((bf16[1,1536,192]{1,2,0:T(8,128)(2,1)}), bf16[1,768,192]{1,2,0:T(8,128)(2,1)}) %reduce-scatter.41.cloned.1.call-update) | async-done | bytes 294928 | tf_op jit(solution)/shard_map/reduce_scatter | solution.py:226
  662.1 17.8 %reduce-scatter.57.cloned.1.call-done = bf16[384,768]{1,0:T(8,128)(2,1)} async-done(((bf16[768,768]{1,0:T(8,128)(2,1)}), bf16[384,768]{1,0:T(8,128)(2,1)}) %reduce-scatter.57.cloned.1.call-update) | async-done | bytes 589840
  682.0 19.8 %reduce-scatter.49.cloned.1.call-done = bf16[384,576]{1,0:T(8,128)(2,1)} async-done(((bf16[768,576]{1,0:T(8,128)(2,1)}), bf16[384,576]{1,0:T(8,128)(2,1)}) %reduce-scatter.49.cloned.1.call-update) | async-done | bytes 442384
  706.4 19.9 %reduce-scatter.47.cloned.1.call-done = bf16[384,768]{1,0:T(8,128)(2,1)} async-done(((bf16[768,768]{1,0:T(8,128)(2,1)}), bf16[384,768]{1,0:T(8,128)(2,1)}) %reduce-scatter.47.cloned.1.call-update) | async-done | bytes 589840 | tf_op jit(solution)/shard_map/reduce_scatter | solution.py:255
  726.3 24.6 %reduce-scatter.45.cloned.1.call-done = bf16[384,768]{1,0:T(8,128)(2,1)} async-done(((bf16[768,768]{1,0:T(8,128)(2,1)}), bf16[384,768]{1,0:T(8,128)(2,1)}) %reduce-scatter.45.cloned.1.call-update) | async-done | bytes 589840 | tf_op jit(solution)/shard_map/reduce_scatter | solution.py:255
  765.6 11.6 %reduce-scatter.67.cloned.1.call-done = bf16[384,4]{1,0:T(8,128)(2,1)} async-done(((bf16[768,4]{1,0:T(8,128)(2,1)}), bf16[384,4]{1,0:T(8,128)(2,1)}) %reduce-scatter.67.cloned.1.call-update) | async-done | bytes 3088
  783.2 38.4 %all-reduce = (f32[2,2,192]{2,1,0:T(2,128)}, f32[2,768]{1,0:T(2,128)}) all-reduce(f32[2,2,192]{2,1,0:T(2,128)} %pad_maximum_fusion.13, f32[2,768]{1,0:T(2,128)} %pad_maximum_fusion.10), channel_id=1, replica_groups=mesh['dp'=4,'seq'=2,'head'=4] {'dp','seq'}, use_global_device_ids=true, to_apply=%region_42.43 | all-reduce | flops 2304 | bytes 18432 | tf_op jit(solution)/shard_map/psum | solution.py:291
  831.0 11.4 %all-reduce.2 = (bf16[1,2,384]{2,1,0:T(2,128)(2,1)S(1)}, bf16[1,2,384]{2,1,0:T(2,128)(2,1)S(1)}, bf16[1,4,384]{2,1,0:T(4,128)(2,1)S(1)}, bf16[1,4,384]{2,1,0:T(4,128)(2,1)S(1)}) all-reduce(bf16[1,2,384]{2,1,0:T(2,128)(2,1)S(1)} %bitcast.337, bf16[1,2,384]{2,1,0:T(2,128)(2,1)S(1)} %bitcast.338, ...), channel_id=1, replica_groups=mesh['dp'=4,'seq'=2,'head'=4] {'dp'}, use_global_device_ids=true, to_apply=%region_65.66 | all-reduce | flops 4608 | bytes 18432 | tf_op jit(solution)/shard_map/psum | solution.py:273
  843.6 45.2 %all-reduce.27.cloned.1.call-done = (bf16[1,3,384,192]{2,3,1,0:T(8,128)(2,1)}, bf16[1,3,384,192]{2,3,1,0:T(8,128)(2,1)}, bf16[1,192,384]{2,1,0:T(8,128)(2,1)}, b...) async-done(((bf16[1,3,384,192]{2,3,1,0:T(8,128)(2,1)}, ...) | async-done | bytes 3538960 | tf_op jit(solution)/shard_map/psum | solution.py:269
  (528 shorter events, 365.0 us)
Async XLA Ops:
  8.1 138.5 %all-reduce.13.cloned.1.call-start = ((), (), s32[]{:S(2)}) async-start(), calls=%async_computation.16 | async-start | bytes 4718592 | tf_op jit(solution)/shard_map/psum | solution.py:136
  90.2 68.0 %all-gather.19.cloned.1.call-start = ((), (), s32[]{:S(2)}) async-start(), calls=%async_computation.29 | async-start | bytes 1769472 | tf_op jit(solution)/shard_map/all_gather | solution.py:112
  91.8 107.8 %all-reduce.15.cloned.1.call-start = ((), (), s32[]{:S(2)}) async-start(), calls=%async_computation.17 | async-start | bytes 2359296 | tf_op jit(solution)/shard_map/psum | solution.py:162
  162.1 147.6 %all-reduce.17.cloned.1.call-start = ((), (), s32[]{:S(2)}) async-start(), calls=%async_computation.18 | async-start | bytes 4718592 | tf_op jit(solution)/shard_map/psum | solution.py:136
  254.0 69.3 %all-gather.23.cloned.1.call-start = ((), (), s32[]{:S(2)}) async-start(), calls=%async_computation.31 | async-start | bytes 1769472 | tf_op jit(solution)/shard_map/all_gather | solution.py:112
  254.7 114.4 %all-reduce.19.cloned.1.call-start = ((), (), s32[]{:S(2)}) async-start(), calls=%async_computation.19 | async-start | bytes 2359296 | tf_op jit(solution)/shard_map/psum | solution.py:209
  331.7 83.9 %reduce-scatter.39.cloned.1.call-start = ((), (), s32[]{:S(2)}) async-start(), calls=%async_computation.21 | async-start | bytes 884736 | tf_op jit(solution)/shard_map/reduce_scatter | solution.py:229
  408.9 60.3 %all-reduce.21.cloned.1.call-start = ((), (), s32[]{:S(2)}) async-start(), calls=%async_computation.22 | async-start | bytes 2359296 | tf_op jit(solution)/shard_map/psum | solution.py:242
  431.7 87.3 %all-reduce.23.cloned.1.call-start = ((), (), s32[]{:S(2)}) async-start(), calls=%async_computation.23 | async-start | bytes 2359296 | tf_op jit(solution)/shard_map/psum | solution.py:209
  481.3 79.7 %reduce-scatter.43.cloned.1.call-start = ((), (), s32[]{:S(2)}) async-start(), calls=%async_computation.25 | async-start | bytes 884736 | tf_op jit(solution)/shard_map/reduce_scatter | solution.py:229
  554.4 84.2 %all-reduce.25.cloned.1.call-start = ((), (), s32[]{:S(2)}) async-start(), calls=%async_computation.42 | async-start | bytes 4718592 | tf_op jit(solution)/shard_map/psum | solution.py:162
  576.5 75.3 %reduce-scatter.55.cloned.1.call-start = ((), (), s32[]{:S(2)}) async-start(), calls=%async_computation.35 | async-start | bytes 589824
  581.7 71.8 %reduce-scatter.59.cloned.1.call-start = ((), (), s32[]{:S(2)}) async-start(), calls=%async_computation.37 | async-start | bytes 1769472
  587.8 67.9 %reduce-scatter.53.cloned.1.call-start = ((), (), s32[]{:S(2)}) async-start(), calls=%async_computation.34 | async-start | bytes 589824
  589.2 68.2 %reduce-scatter.51.cloned.1.call-start = ((), (), s32[]{:S(2)}) async-start(), calls=%async_computation.33 | async-start | bytes 1474560
  597.6 82.3 %reduce-scatter.57.cloned.1.call-start = ((), (), s32[]{:S(2)}) async-start(), calls=%async_computation.36 | async-start | bytes 1769472
  602.4 99.4 %reduce-scatter.49.cloned.1.call-start = ((), (), s32[]{:S(2)}) async-start(), calls=%async_computation.32 | async-start | bytes 1474560
  610.4 115.9 %reduce-scatter.47.cloned.1.call-start = ((), (), s32[]{:S(2)}) async-start(), calls=%async_computation.27 | async-start | bytes 1769472 | tf_op jit(solution)/shard_map/reduce_scatter | solution.py:255
  614.3 136.6 %reduce-scatter.45.cloned.1.call-start = ((), (), s32[]{:S(2)}) async-start(), calls=%async_computation.26 | async-start | bytes 1769472 | tf_op jit(solution)/shard_map/reduce_scatter | solution.py:255
  618.8 145.3 %reduce-scatter.63.cloned.1.call-start = ((), (), s32[]{:S(2)}) async-start(), calls=%async_computation.39 | async-start | bytes 294912
  629.7 147.5 %reduce-scatter.67.cloned.1.call-start = ((), (), s32[]{:S(2)}) async-start(), calls=%async_computation.41 | async-start | bytes 294912
  633.9 195.0 %reduce-scatter.61.cloned.1.call-start = ((), (), s32[]{:S(2)}) async-start(), calls=%async_computation.38 | async-start | bytes 294912
  648.8 181.2 %reduce-scatter.65.cloned.1.call-start = ((), (), s32[]{:S(2)}) async-start(), calls=%async_computation.40 | async-start | bytes 294912
  651.7 237.0 %all-reduce.27.cloned.1.call-start = ((), (), s32[]{:S(2)}) async-start(), calls=%async_computation.43 | async-start | bytes 7077888 | tf_op jit(solution)/shard_map/psum | solution.py:269
  (142 other events, 1517.2 us)
Sparse Core Ops, SparseCore 0:
  89.1 57.3 all-reduce.12
  162.2 37.3 all-reduce.14
  253.5 56.0 all-reduce.16
  331.8 37.3 all-reduce.18
  431.8 37.2 all-reduce.20
  481.5 37.5 all-reduce.22
  576.6 55.8 all-reduce.24
  751.1 137.6 all-reduce.26
Sparse Core Ops, SparseCore 1:
  91.6 24.3 all-gather.16
  118.0 22.6 all-gather.18
  256.0 23.1 all-gather.20
  280.7 22.6 all-gather.22
  395.1 15.3 reduce-scatter.38
  412.8 15.2 reduce-scatter.36
  540.5 15.3 reduce-scatter.42
  558.0 15.2 reduce-scatter.40
  581.8 13.0 reduce-scatter.54
  597.3 21.6 reduce-scatter.58
  621.1 13.0 reduce-scatter.52
  636.6 19.5 reduce-scatter.50
  658.2 21.6 reduce-scatter.56
  682.3 19.5 reduce-scatter.48
  704.6 21.6 reduce-scatter.46
  729.2 21.6 reduce-scatter.44
  753.2 10.9 reduce-scatter.62
  766.3 10.9 reduce-scatter.66
  779.4 11.0 reduce-scatter.60
  792.7 11.0 reduce-scatter.64
where the time goes:
time: 914 us; the launch traced here: 904 us
  waiting for transfers between devices  402 us (44%)
  matrix products  144 us (16%)
  blocking collectives  133 us (15%)
  other arithmetic  110 us (12%)
  local copies, waits for them, and re-layouts  92.4 us (10%)
  between operations  18.7 us (2%)
    psum x2, waiting for transfers between devices, on_device(): mid = stream + lax.psum(attn_part, 'head') + shift_set[1]  108 us
    psum x2, waiting for transfers between devices, on_device(): lax.psum(jnp.dot(d_hidden, up_full.T, preferred_element_type=jnp.float32)...  73.1 us
    unnamed x300, local copies, waits for them, and re-layouts  60.8 us
    unnamed x38, waiting for transfers between devices  57.2 us
    psum x1, waiting for transfers between devices, on_device(): lax.psum(share_qkv.astype(jnp.bfloat16), 'dp').astype(jnp.float32)  45.2 us
    reduce_scatter x2, waiting for transfers between devices, on_device(): lax.psum_scatter(d_up.astype(jnp.bfloat16), 'seq', scatter_dimension=0, t...  44.5 us
    psum x1, blocking collectives, on_device(): lax.psum((stack_member(bias_grads, 0), stack_member(bias_grads, 1)), ('dp...  38.4 us
    psum x1, waiting for transfers between devices, on_device(): lax.psum(d_normed_part.astype(jnp.bfloat16), 'head').astype(jnp.float32)  37.2 us
  transfers between devices with their start and end apart: 28, of which 15 were waited for; matrix products, arithmetic and copies ran while one was open for 20% of the time, Pallas kernels for 0%

commit v1 on v0

v1 whole, which is shorter than its diff:
```python
import functools

import jax
import jax.numpy as jnp
from jax import lax
from jax.experimental import pallas as pl
from jax.experimental.pallas import tpu as pltpu
from jax.sharding import PartitionSpec as P

HD = 64


epsilon = 1e-05


def normalize(values, gain_vector, shift_vector):
    row_mean = jnp.mean(values, axis=-1, keepdims=True)
    centered = values - row_mean
    variance = jnp.mean(centered * centered, axis=-1, keepdims=True)
    return centered * lax.rsqrt(variance + epsilon) * gain_vector + shift_vector


def gelu_exact(values):
    return jax.nn.gelu(values, approximate=False)


def column_sum(values):
    return jnp.sum(values.astype(jnp.float32), axis=0)


def stack_member(collected, position):
    return jnp.stack([entry[position] for entry in collected])


NT = (((1,), (1,)), ((), ()))
NN = (((1,), (0,)), ((), ()))
VMEM = pl.BlockSpec(memory_space=pltpu.VMEM)
BIG = 48 * 1024 * 1024


def head_masks(shape, heads):
    column = lax.broadcasted_iota(jnp.int32, shape, 1)
    return [(column >= h * HD) & (column < (h + 1) * HD) for h in range(heads)]


def attend_kernel(heads, q_ref, k_ref, v_ref, bias_ref, out_ref, lse_ref, vt_ref):
    @pl.when(pl.program_id(0) == 0)
    def _():
        vt_ref[...] = v_ref[...].astype(jnp.float32).T.astype(jnp.bfloat16)

    queries = q_ref[...]
    zero = jnp.zeros_like(queries)
    parts = []
    for h, mask in enumerate(head_masks(queries.shape, heads)):
        scores = lax.dot_general(
            k_ref[...], jnp.where(mask, queries, zero), NT, preferred_element_type=jnp.float32
        )
        scores = scores + bias_ref[...]
        peak = jnp.max(scores, axis=0, keepdims=True)
        powered = jnp.exp(scores - peak)
        total = jnp.sum(powered, axis=0, keepdims=True)
        probs = (powered * (1.0 / total)).astype(jnp.bfloat16)
        parts.append(
            lax.dot_general(
                vt_ref[h * HD : (h + 1) * HD, :], probs, NN, preferred_element_type=jnp.float32
            )
        )
        lse_ref[0, h : h + 1, :] = peak + jnp.log(total)
    out_ref[...] = jnp.concatenate(parts, axis=0).T.astype(jnp.bfloat16)


def row_block(rows):
    return 256 if rows % 256 == 0 else rows


def attend(queries, key_all, value_all, bias):
    rows, width = queries.shape
    keys = key_all.shape[0]
    heads = width // HD
    block = row_block(rows)
    return pl.pallas_call(
        functools.partial(attend_kernel, heads),
        grid=(rows // block,),
        in_specs=[
            pl.BlockSpec((block, width), lambda i: (i, 0)),
            pl.BlockSpec((keys, width), lambda i: (0, 0)),
            pl.BlockSpec((keys, width), lambda i: (0, 0)),
            pl.BlockSpec((keys, 1), lambda i: (0, 0)),
        ],
        out_specs=[
            pl.BlockSpec((block, width), lambda i: (i, 0)),
            pl.BlockSpec((1, heads, block), lambda i: (i, 0, 0)),
        ],
        out_shape=[
            jax.ShapeDtypeStruct((rows, width), jnp.bfloat16),
            jax.ShapeDtypeStruct((rows // block, heads, block), jnp.float32),
        ],
        scratch_shapes=[pltpu.VMEM((width, keys), jnp.bfloat16)],
        compiler_params=pltpu.CompilerParams(vmem_limit_bytes=BIG),
        cost_estimate=pl.CostEstimate(
            flops=8 * rows * keys * width, bytes_accessed=6 * keys * width, transcendentals=rows * keys * heads
        ),
    )(queries, key_all, value_all, bias)


def attend_back_kernel(
    heads, q_ref, k_ref, v_ref, bias_ref, lse_ref, o_ref, do_ref,
    dq_ref, dk_ref, dv_ref, kt_ref, dk_sum, dv_sum,
):
    step = pl.program_id(0)

    @pl.when(step == 0)
    def _():
        kt_ref[...] = k_ref[...].astype(jnp.float32).T.astype(jnp.bfloat16)
        dk_sum[...] = jnp.zeros_like(dk_sum)
        dv_sum[...] = jnp.zeros_like(dv_sum)

    queries = q_ref[...]
    grads = do_ref[...]
    zero = jnp.zeros_like(queries)
    inner = (o_ref[...].astype(jnp.float32) * grads.astype(jnp.float32)).T
    parts = []
    for h, mask in enumerate(head_masks(queries.shape, heads)):
        q_head = jnp.where(mask, queries, zero)
        do_head = jnp.where(mask, grads, zero)
        delta = jnp.sum(inner[h * HD : (h + 1) * HD, :], axis=0, keepdims=True)
        scores = lax.dot_general(k_ref[...], q_head, NT, preferred_element_type=jnp.float32)
        probs = jnp.exp(scores + bias_ref[...] - lse_ref[0, h : h + 1, :])
        d_probs = lax.dot_general(v_ref[...], do_head, NT, preferred_element_type=jnp.float32)
        dv_sum[...] += jnp.dot(
            probs.astype(jnp.bfloat16), do_head, preferred_element_type=jnp.float32
        )
        d_scores = (probs * (d_probs - delta)).astype(jnp.bfloat16)
        dk_sum[...] += jnp.dot(d_scores, q_head, preferred_element_type=jnp.float32)
        parts.append(
            jnp.dot(
                kt_ref[h * HD : (h + 1) * HD, :], d_scores, preferred_element_type=jnp.float32
            )
        )
    d_query = jnp.concatenate(parts, axis=0).T.astype(jnp.bfloat16)
    dq_ref[...] = (d_query.astype(jnp.float32) * (HD ** (-0.5))).astype(jnp.bfloat16)

    @pl.when(step == pl.num_programs(0) - 1)
    def _():
        dk_ref[...] = dk_sum[...].astype(jnp.bfloat16)
        dv_ref[...] = dv_sum[...].astype(jnp.bfloat16)


def attend_back(queries, key_all, value_all, bias, logsum, attended, d_attended):
    rows, width = queries.shape
    keys = key_all.shape[0]
    heads = width // HD
    block = row_block(rows)
    row_spec = pl.BlockSpec((block, width), lambda i: (i, 0))
    key_spec = pl.BlockSpec((keys, width), lambda i: (0, 0))
    return pl.pallas_call(
        functools.partial(attend_back_kernel, heads),
        grid=(rows // block,),
        in_specs=[
            row_spec,
            key_spec,
            key_spec,
            pl.BlockSpec((keys, 1), lambda i: (0, 0)),
            pl.BlockSpec((1, heads, block), lambda i: (i, 0, 0)),
            row_spec,
            row_spec,
        ],
        out_specs=[row_spec, key_spec, key_spec],
        out_shape=[
            jax.ShapeDtypeStruct((rows, width), jnp.bfloat16),
            jax.ShapeDtypeStruct((keys, width), jnp.bfloat16),
            jax.ShapeDtypeStruct((keys, width), jnp.bfloat16),
        ],
        scratch_shapes=[
            pltpu.VMEM((width, keys), jnp.bfloat16),
            pltpu.VMEM((keys, width), jnp.float32),
            pltpu.VMEM((keys, width), jnp.float32),
        ],
        compiler_params=pltpu.CompilerParams(vmem_limit_bytes=BIG),
        cost_estimate=pl.CostEstimate(
            flops=20 * rows * keys * width, bytes_accessed=12 * keys * width, transcendentals=rows * keys * heads
        ),
    )(queries, key_all, value_all, bias, logsum, attended, d_attended)


def head_sum_kernel(dims, chunks, a_ref, w_ref, out_ref, first, landed, own, chip, crossed, last, done, send, recv):
    me = lax.axis_index("head")
    core = me % 2
    sibling = me + 1 - 2 * core
    across = (me + 2) % 4
    half = a_ref.shape[0] // 2
    size = half // chunks
    mine = core * half
    theirs = (1 - core) * half

    barrier = pltpu.get_barrier_semaphore()
    for other in (sibling, across):
        pl.semaphore_signal(
            barrier, inc=1, device_id={"head": other}, device_id_type=pl.DeviceIdType.MESH
        )

    def product(base):
        rows = pl.ds(pl.multiple_of(base, 16), size)
        return lax.dot_general(a_ref[rows, :], w_ref[...], dims, preferred_element_type=jnp.float32)

    def remote(source, target, stage, c, other):
        return pltpu.make_async_remote_copy(
            src_ref=source.at[c],
            dst_ref=target.at[c],
            send_sem=send.at[stage, c],
            recv_sem=recv.at[stage, c],
            device_id={"head": other},
            device_id_type=pl.DeviceIdType.MESH,
        )

    outward = [remote(first, landed, 0, c, sibling) for c in range(chunks)]
    cross = [remote(chip, crossed, 1, c, across) for c in range(chunks)]
    back = [remote(last, done, 2, c, sibling) for c in range(chunks)]
    for c in range(chunks):
        first[c] = product(theirs + c * size).astype(jnp.bfloat16)
        if c == 0:
            pl.semaphore_wait(barrier, 2)
        outward[c].start()
    for c in range(chunks):
        own[c] = product(mine + c * size)
        outward[c].wait_recv()
        chip[c] = (own[c] + landed[c].astype(jnp.float32)).astype(jnp.bfloat16)
        cross[c].start()
    for c in range(chunks):
        cross[c].wait_recv()
        total = (chip[c].astype(jnp.float32) + crossed[c].astype(jnp.float32)).astype(jnp.bfloat16)
        last[c] = total
        back[c].start()
        out_ref[pl.ds(pl.multiple_of(mine + c * size, 16), size), :] = total
    for c in range(chunks):
        back[c].wait_recv()
        out_ref[pl.ds(pl.multiple_of(theirs + c * size, 16), size), :] = done[c]
    for c in range(chunks):
        outward[c].wait_send()
        cross[c].wait_send()
        back[c].wait_send()


def head_sum(a, w, transposed, call_id):
    rows = a.shape[0]
    columns = w.shape[0] if transposed else w.shape[1]
    chunks = 3
    piece = (chunks, rows // 2 // chunks, columns)
    low = pltpu.VMEM(piece, jnp.bfloat16)
    return pl.pallas_call(
        functools.partial(head_sum_kernel, NT if transposed else NN, chunks),
        in_specs=[VMEM, VMEM],
        out_specs=VMEM,
        out_shape=jax.ShapeDtypeStruct((rows, columns), jnp.bfloat16),
        scratch_shapes=[
            low, low, pltpu.VMEM(piece, jnp.float32), low, low, low, low,
            pltpu.SemaphoreType.DMA((3, chunks)),
            pltpu.SemaphoreType.DMA((3, chunks)),
        ],
        compiler_params=pltpu.CompilerParams(
            collective_id=call_id, has_side_effects=True, vmem_limit_bytes=BIG
        ),
        cost_estimate=pl.CostEstimate(
            flops=2 * rows * columns * a.shape[1], bytes_accessed=40 * rows * columns, transcendentals=0
        ),
    )(a, w)


def swap(values):
    return lax.ppermute(values, "seq", [(0, 1), (1, 0)])


def gather_seq(values, axis):
    if lax.axis_size("seq") != 2:
        return lax.all_gather(values, "seq", axis=axis, tiled=True)
    other = swap(values)
    first = lax.axis_index("seq") == 0
    return jnp.concatenate(
        [jnp.where(first, values, other), jnp.where(first, other, values)], axis=axis
    )


def scatter_seq(values, axis):
    if lax.axis_size("seq") != 2:
        return lax.psum_scatter(
            values.astype(jnp.bfloat16), "seq", scatter_dimension=axis, tiled=True
        )
    size = values.shape[axis] // 2
    me = lax.axis_index("seq")
    kept = lax.dynamic_slice_in_dim(values, me * size, size, axis)
    sent = lax.dynamic_slice_in_dim(values, (1 - me) * size, size, axis)
    return (kept + swap(sent.astype(jnp.bfloat16)).astype(jnp.float32)).astype(jnp.bfloat16)


def own_part(values):
    size = values.shape[-1] // lax.axis_size("seq")
    return lax.dynamic_slice_in_dim(values, lax.axis_index("seq") * size, size, values.ndim - 1)


def on_device(
    frames, lengths, grad_out, w_qkv, qv_bias, w_out, w_up, up_bias, w_down, gains, shifts
):
    clip_count, rows_dev, model_width = frames.shape
    row_count = clip_count * rows_dev
    layers = w_qkv.shape[0]
    head_width = w_qkv.shape[3]
    query_scale = HD ** (-0.5)
    parts = lax.axis_size("seq")
    me = lax.axis_index("seq")
    key_length = rows_dev * parts
    positions = jnp.arange(key_length, dtype=jnp.int32)
    if parts == 2:
        positions = (positions + me * rows_dev) % key_length
    bias = jnp.where(positions < lengths[0], 0.0, -1e30).astype(jnp.float32)[:, None]

    vectors = gather_seq(jnp.concatenate([gains, shifts], axis=1), 2).astype(jnp.float32)
    gain_all, shift_all = vectors[:, :2], vectors[:, 2:]
    weights = []
    for l in range(layers):
        qkv = gather_seq(w_qkv[l], 1)
        weights.append(
            (
                qkv.transpose(1, 0, 2).reshape(model_width, 3 * head_width),
                gather_seq(w_out[l], 1),
                gather_seq(w_up[l], 0),
                gather_seq(w_down[l], 1),
            )
        )

    stream = frames.astype(jnp.float32).reshape(row_count, model_width)
    saved_layers = []
    for l in range(layers):
        qkv_full, out_full, up_full, down_full = weights[l]
        gain_pair, shift_set = gain_all[l], shift_all[l]
        bias_pair = qv_bias[l].astype(jnp.float32)
        normed = normalize(stream, gain_pair[0], shift_set[0]).astype(jnp.bfloat16)
        pair = jnp.dot(normed, qkv_full[:, head_width:], preferred_element_type=jnp.float32)
        pair = pair + jnp.concatenate([jnp.zeros_like(bias_pair[1]), bias_pair[1]])
        pair = pair.astype(jnp.bfloat16)
        if parts == 2:
            pair_all = jnp.concatenate([pair, swap(pair)], axis=0)
        else:
            pair_all = lax.all_gather(pair, "seq", axis=0, tiled=True)
        key_all, value_all = pair_all[:, :head_width], pair_all[:, head_width:]
        queries = jnp.dot(normed, qkv_full[:, :head_width], preferred_element_type=jnp.float32)
        queries = ((queries + bias_pair[0]) * query_scale).astype(jnp.bfloat16)
        attended, logsum = attend(queries, key_all, value_all, bias)
        mid = stream + head_sum(attended, out_full, False, 1).astype(jnp.float32) + shift_set[1]
        normed_two = normalize(mid, gain_pair[1], shift_set[2]).astype(jnp.bfloat16)
        hidden_pre = jnp.dot(normed_two, up_full, preferred_element_type=jnp.float32) + up_bias[
            l
        ].astype(jnp.float32)
        activated = gelu_exact(hidden_pre).astype(jnp.bfloat16)
        saved_layers.append(
            (stream, mid, normed, queries, key_all, value_all, logsum, attended, normed_two, hidden_pre, activated)
        )
        stream = (
            mid + head_sum(activated, down_full, False, 2).astype(jnp.float32) + shift_set[3]
        )
    output = stream.astype(jnp.bfloat16).reshape(clip_count, rows_dev, model_width)

    grad_stream = grad_out.astype(jnp.float32).reshape(row_count, model_width)
    owned = [None] * layers
    small = [None] * layers
    for l in range(layers - 1, -1, -1):
        (
            stream_in, mid, normed, queries, key_all, value_all,
            logsum, attended, normed_two, hidden_pre, activated,
        ) = saved_layers[l]
        qkv_full, out_full, up_full, down_full = weights[l]
        gain_pair, shift_set = gain_all[l], shift_all[l]
        grad_low = grad_stream.astype(jnp.bfloat16)
        d_shift_mlp = column_sum(grad_low)
        d_act = jnp.dot(grad_low, down_full.T, preferred_element_type=jnp.float32)
        gelu_value, gelu_pull = jax.vjp(gelu_exact, hidden_pre)
        d_hidden = gelu_pull(d_act)[0].astype(jnp.bfloat16)
        d_up_bias = column_sum(d_hidden)
        d_norm_two = head_sum(d_hidden, up_full, True, 3).astype(jnp.float32)
        share_down = scatter_seq(
            jnp.dot(activated.T, grad_low, preferred_element_type=jnp.float32), 1
        )
        share_up = scatter_seq(
            jnp.dot(normed_two.T, d_hidden, preferred_element_type=jnp.float32), 0
        )
        norm_value, norm_pull = jax.vjp(normalize, mid, gain_pair[1], shift_set[2])
        d_mid, d_gain_two, d_shift_two = norm_pull(d_norm_two)
        grad_stream = grad_stream + d_mid
        grad_low = grad_stream.astype(jnp.bfloat16)
        d_shift_attn = column_sum(grad_low)
        d_attended = jnp.dot(grad_low, out_full.T, preferred_element_type=jnp.float32).astype(
            jnp.bfloat16
        )
        d_query, d_key_part, d_value_part = attend_back(
            queries, key_all, value_all, bias, logsum, attended, d_attended
        )
        d_pair = jnp.concatenate([d_key_part, d_value_part], axis=1)
        if parts == 2:
            d_pair = (
                d_pair[:rows_dev].astype(jnp.float32) + swap(d_pair[rows_dev:]).astype(jnp.float32)
            ).astype(jnp.bfloat16)
        else:
            d_pair = lax.psum_scatter(d_pair, "seq", scatter_dimension=0, tiled=True)
        share_out = scatter_seq(
            jnp.dot(attended.T, grad_low, preferred_element_type=jnp.float32), 1
        )
        d_qkv = jnp.concatenate([d_query, d_pair], axis=1)
        d_normed = head_sum(d_qkv, qkv_full, True, 4).astype(jnp.float32)
        d_qkv_weight = jnp.dot(normed.T, d_qkv, preferred_element_type=jnp.float32)
        share_qkv = scatter_seq(d_qkv_weight, 0)
        share_qkv = share_qkv.reshape(-1, 3, head_width).transpose(1, 0, 2)
        d_bias = column_sum(d_qkv)
        norm_value, norm_pull = jax.vjp(normalize, stream_in, gain_pair[0], shift_set[0])
        d_before, d_gain_one, d_shift_one = norm_pull(d_normed)
        grad_stream = grad_stream + d_before
        owned[l] = (share_qkv, share_out, share_up, share_down)
        small[l] = (
            jnp.stack([d_bias[:head_width], d_bias[2 * head_width :]]),
            d_up_bias,
            jnp.stack([d_gain_one, d_gain_two]),
            jnp.stack([d_shift_one, d_shift_attn, d_shift_two, d_shift_mlp]),
        )
    owned = lax.psum(owned, "dp")
    grad_qkv, grad_out_weight, grad_up_weight, grad_down_weight = (
        stack_member(owned, p).astype(jnp.float32) for p in range(4)
    )
    grad_bias_pair, grad_bias_up, grad_gain_set, grad_shift_set = lax.psum(
        tuple(stack_member(small, p) for p in range(4)), ("dp", "seq")
    )
    grad_frames = grad_stream.reshape(clip_count, rows_dev, model_width)
    return (
        output,
        grad_frames,
        grad_qkv,
        grad_bias_pair,
        grad_out_weight,
        grad_up_weight,
        grad_bias_up,
        grad_down_weight,
        own_part(grad_gain_set),
        own_part(grad_shift_set),
    )


def solution(mesh):
    return jax.shard_map(
        on_device,
        mesh=mesh,
        in_specs=(
            P("dp", "seq", None),
            P("dp"),
            P("dp", "seq", None),
            P(None, None, "seq", "head"),
            P(None, None, "head"),
            P(None, "head", "seq"),
            P(None, "seq", "head"),
            P(None, "head"),
            P(None, "head", "seq"),
            P(None, None, "seq"),
            P(None, None, "seq"),
        ),
        out_specs=(
            P("dp", "seq", None),
            P("dp", "seq", None),
            P(None, None, "seq", "head"),
            P(None, None, "head"),
            P(None, "head", "seq"),
            P(None, "seq", "head"),
            P(None, "head"),
            P(None, "head", "seq"),
            P(None, None, "seq"),
            P(None, None, "seq"),
        ),
        check_vma=False,
    )
```

time: 914 us -> 598 us (0.65)
  waiting for transfers between devices: 402 us -> 175 us
  Pallas kernels: 0 us -> 189 us
  matrix products: 144 us -> 39 us
  blocking collectives: 133 us -> 41.3 us
  local copies, waits for them, and re-layouts: 92.4 us -> 45.5 us
  other arithmetic: 110 us -> 66 us
  starting transfers between devices: 2.73 us -> 19.9 us
    psum x8 -> x1, waiting for transfers between devices: 276 us -> 62 us  [on_device(): owned = lax.psum(owned, 'dp')]
    pallas_call x0 -> x12, Pallas kernels: none -> 189 us  [the longest x8 148 us: head_sum(): pl.pallas_call(functools.partial(head_sum_kernel, NT if transposed else N...]
    ppermute x0 -> x21, waiting for transfers between devices: none -> 113 us  [swap(): return lax.ppermute(values, 'seq', [(0, 1), (1, 0)])]
    dot_general x28 -> x12, matrix products: 116 us -> 16.5 us  [the longest x2 4.27 us: on_device(): jnp.dot(normed_two.T, d_hidden, preferred_element_type=jnp.float32)]
    all_gather x12 -> x0, blocking collectives: 83.3 us -> none  [the longest x2 19 us: on_device(): lax.all_gather(w_qkv[layer_index], 'seq', axis=1, tiled=True)]
    reduce_scatter x6 -> x0, waiting for transfers between devices: 69.1 us -> none  [the longest x2 44.5 us: on_device(): lax.psum_scatter(d_up.astype(jnp.bfloat16), 'seq', scatter_dimension=0, t...]
    unnamed x38 -> x1, waiting for transfers between devices: 57.2 us -> 0.02 us
    unnamed x300 -> x318, local copies, waits for them, and re-layouts: 60.8 us -> 19.8 us
  transfers between devices with their start and end apart: 28 -> 22, of which waited for: 15 -> 11; matrix products, arithmetic and copies ran while one was open for 20% -> 14% of each run, Pallas kernels for 0% -> 11%
where the time goes in v1:
time: 598 us; the launch traced here: 592 us
  Pallas kernels  189 us (32%)
  waiting for transfers between devices  175 us (29%)
  other arithmetic  66 us (11%)
  local copies, waits for them, and re-layouts  45.5 us (8%)
  blocking collectives  41.3 us (7%)
  matrix products  39 us (7%)
  starting transfers between devices  19.9 us (3%)
  between operations  16.8 us (3%)
    pallas_call x8, Pallas kernels, head_sum(): pl.pallas_call(functools.partial(head_sum_kernel, NT if transposed else N...  148 us
    ppermute x21, waiting for transfers between devices, swap(): return lax.ppermute(values, 'seq', [(0, 1), (1, 0)])  113 us
    psum x1, waiting for transfers between devices, on_device(): owned = lax.psum(owned, 'dp')  62 us
    psum x1, blocking collectives, on_device(): lax.psum(tuple((stack_member(small, p) for p in range(4))), ('dp', 'seq'))  41.3 us
    pallas_call x2, Pallas kernels, attend_back(): pl.pallas_call(functools.partial(attend_back_kernel, heads), grid=(rows /...  21 us
    pallas_call x2, Pallas kernels, attend(): pl.pallas_call(functools.partial(attend_kernel, heads), grid=(rows // blo...  20 us
    ppermute x21, starting transfers between devices, swap(): return lax.ppermute(values, 'seq', [(0, 1), (1, 0)])  19.8 us
    unnamed x318, local copies, waits for them, and re-layouts  19.8 us
  transfers between devices with their start and end apart: 22, of which 11 were waited for; matrix products, arithmetic and copies ran while one was open for 14% of the time, Pallas kernels for 11%

profile of v1, /device:TPU:0, one launch (start us, length us, event | category | flops | bytes accessed | tf_op | source)
XLA Modules:
  0.0 592.2 jit_solution(7736127641732659340)
XLA Ops:
  27.3 12.0 %collective-permute-done.3 = bf16[192,384]{1,0:T(8,128)(2,1)} collective-permute-done((bf16[192,384]{1,0:T(8,128)(2,1)}, bf16[192,384]{1,0:T(8,128)(2,1)}, u32[]{:S(2)}, u32[]{:S(2)}) %collective-permute-start.3) | collective-permute-done | bytes 147488 | tf_op jit(solution)/shard_map/ppermute | solution.py:270
  49.5 30.8 %collective-permute-done.10 = bf16[768,384]{1,0:T(8,128)(2,1)S(1)} collective-permute-done((bf16[768,384]{1,0:T(8,128)(2,1)S(1)}, bf16[768,384]{1,0:T(8,128)(2,1)S(1)}, u32[]{:S(2)}, u32[]{:S(2)}) %collective-permute-start.10) | collective-permute-done | bytes 589856 | tf_op jit(solution)/shard_map/ppermute | solution.py:270
  80.2 12.6 %collective-permute-done.5 = bf16[768,384]{1,0:T(8,128)(2,1)S(1)} collective-permute-done((bf16[768,384]{1,0:T(8,128)(2,1)S(1)}, bf16[768,384]{1,0:T(8,128)(2,1)S(1)}, u32[]{:S(2)}, u32[]{:S(2)}) %collective-permute-start.5) | collective-permute-done | bytes 589856 | tf_op jit(solution)/shard_map/ppermute | solution.py:270
  96.4 7.6 %collective-permute-done.2 = bf16[768,384]{1,0:T(8,128)(2,1)S(1)} collective-permute-done((bf16[768,384]{1,0:T(8,128)(2,1)S(1)}, bf16[768,384]{1,0:T(8,128)(2,1)S(1)}, u32[]{:S(2)}, u32[]{:S(2)}) %collective-permute-start.2) | collective-permute-done | bytes 589856 | tf_op jit(solution)/shard_map/ppermute | solution.py:270
  104.5 9.9 %shard_map.186 = (bf16[768,192]{1,0:T(8,128)(2,1)S(1)}, f32[3,3,256]{2,1,0:T(4,128)S(1)}) custom-call(bf16[768,192]{1,0:T(8,128)(2,1)S(1)} %fusion.53.q_ref, bf16[1536,192]{1,0:T(8,128)(2,1)S(1)} %get-tuple-element.112.k_ref, bf16[1536,192]{1,0:T(8,128)(2,1)S(1)} %get-tuple-element.111.v_ref, f32[1536,1]{1,0:T(8,128)S(1)} %fusion.65.bias_ref), custom_call_target="tpu_custom_call" | custom-call | flops 1811939328 | bytes 1769472 | tf_op jit(solution)/shard_map/pallas_call | solution.py:81
  114.4 18.3 %shard_map.187 = bf16[768,768]{1,0:T(8,128)(2,1)S(1)} custom-call(bf16[768,192]{1,0:T(8,128)(2,1)S(1)} %get-tuple-element.20.a_ref.o_ref, bf16[192,768]{1,0:T(8,128)(2,1)S(1)} %get-tuple-element.149.w_ref), custom_call_target="tpu_custom_call" | custom-call | flops 226492416 | bytes 23592960 | tf_op jit(solution)/shard_map/pallas_call | solution.py:250
  133.9 7.9 %multiply_convert_fusion.1 = (bf16[768,768]{1,0:T(8,128)(2,1)S(1)}, f32[768,768]{1,0:T(8,128)}, f32[768,768]{1,0:T(8,128)}) fusion(f32[768]{0:T(1024)S(1)} %copy-done.146, bf16[384,768]{1,0:T(8,128)(2,1)S(1)} %get-tuple-element.105, bf16[384,768]{1,0:T(8,128)(2,1)S(1)} %get-tuple-element.106, f32[768]{0:T(1024)S(1)} %get-tuple-element.52, ...), kind=kOutput, calls=%fused_computation.88 | convolution fusion | flops 952565760 | bytes 9455616 | tf_op jit(solution)/shard_map/dot_general | solution.py:350
  141.9 18.3 %shard_map.188 = bf16[768,768]{1,0:T(8,128)(2,1)S(1)} custom-call(bf16[768,768]{1,0:T(8,128)(2,1)S(1)} %get-tuple-element.85.a_ref, bf16[768,768]{1,0:T(8,128)(2,1)S(1)} %get-tuple-element.151.w_ref), custom_call_target="tpu_custom_call" | custom-call | flops 905969664 | bytes 23592960 | tf_op jit(solution)/shard_map/pallas_call | solution.py:250
  171.3 8.6 %collective-permute-done.7 = bf16[768,384]{1,0:T(8,128)(2,1)} collective-permute-done((bf16[768,384]{1,0:T(8,128)(2,1)}, bf16[768,384]{1,0:T(8,128)(2,1)}, u32[]{:S(2)}, u32[]{:S(2)}) %collective-permute-start.7) | collective-permute-done | bytes 589856 | tf_op jit(solution)/shard_map/ppermute | solution.py:270
  181.7 10.2 %shard_map.189 = (bf16[768,192]{1,0:T(8,128)(2,1)S(1)}, f32[3,3,256]{2,1,0:T(4,128)S(1)}) custom-call(bf16[768,192]{1,0:T(8,128)(2,1)S(1)} %fusion.54.q_ref, bf16[1536,192]{1,0:T(8,128)(2,1)S(1)} %get-tuple-element.110.k_ref, bf16[1536,192]{1,0:T(8,128)(2,1)S(1)} %get-tuple-element.109.v_ref, f32[1536,1]{1,0:T(8,128)S(1)} %copy-done.14), custom_call_target="tpu_custom_call" | custom-call | flops 1811939328 | bytes 1769472 | tf_op jit(solution)/shard_map/pallas_call | solution.py:81
  191.9 18.3 %shard_map.190 = bf16[768,768]{1,0:T(8,128)(2,1)S(1)} custom-call(bf16[768,192]{1,0:T(8,128)(2,1)S(1)} %get-tuple-element.21.a_ref.o_ref, bf16[192,768]{1,0:T(8,128)(2,1)S(1)} %copy-done.12), custom_call_target="tpu_custom_call" | custom-call | flops 226492416 | bytes 23592960 | tf_op jit(solution)/shard_map/pallas_call | solution.py:250
  211.9 7.3 %multiply_convert_fusion = (bf16[768,768]{1,0:T(8,128)(2,1)S(1)}, f32[768,768]{1,0:T(8,128)S(1)}, f32[768,768]{1,0:T(8,128)}) fusion(f32[768]{0:T(1024)S(1)} %copy-done.148, bf16[384,768]{1,0:T(8,128)(2,1)S(1)} %copy-done.61, bf16[384,768]{1,0:T(8,128)(2,1)S(1)} %copy-done.60, f32[768,768]{1,0:T(8,128)S(1)} %get-tuple-element.82, f32[768]{0:T(1024)S(1)} %copy-done.153, ...), kind=kOutput, calls=%fused_computation.69 | convolution fusion | flops 950206464 | bytes 9452544 | tf_op jit(solution)/shard_map/dot_general | solution.py:350
  219.1 18.3 %shard_map.191 = bf16[768,768]{1,0:T(8,128)(2,1)S(1)} custom-call(bf16[768,768]{1,0:T(8,128)(2,1)S(1)} %get-tuple-element.79.a_ref, bf16[768,768]{1,0:T(8,128)(2,1)S(1)} %get-tuple-element.152.w_ref), custom_call_target="tpu_custom_call" | custom-call | flops 905969664 | bytes 23592960 | tf_op jit(solution)/shard_map/pallas_call | solution.py:250
  245.3 18.8 %shard_map.192 = bf16[768,768]{1,0:T(8,128)(2,1)S(1)} custom-call(bf16[768,768]{1,0:T(8,128)(2,1)S(1)} %get-tuple-element.140.a_ref, bf16[768,768]{1,0:T(8,128)(2,1)S(1)} %get-tuple-element.144.w_ref), custom_call_target="tpu_custom_call" | custom-call | flops 905969664 | bytes 23592960 | tf_op jit(solution)/shard_map/pallas_call | solution.py:250
  279.0 10.4 %shard_map.193 = (bf16[768,192]{1,0:T(8,128)(2,1)S(1)}, bf16[1536,192]{1,0:T(8,128)(2,1)S(1)}, bf16[1536,192]{1,0:T(8,128)(2,1)S(1)}) custom-call(bf16[768,192]{1,0:T(8,128)(2,1)S(1)} %copy-done.28, bf16[1536,192]{1,0:T(8,128)(2,1)S(1)} %copy-done.24, bf16[1536,192]{1,0:T(8,128)(2,1)S(1)} %copy-done.22, f32[1536,1]{1,0:T(8,128)S(1)} %copy-done.15, ...), custom_call_target="tpu_custom_call" | custom-call | flops 4529848320 | bytes 3538944 | tf_op jit(solution)/shard_map/pallas_call | solution.py:156
  300.6 8.5 %collective-permute-done.16 = bf16[192,384]{1,0:T(8,128)(2,1)S(1)} collective-permute-done((bf16[192,384]{1,0:T(8,128)(2,1)S(1)}, bf16[192,384]{1,0:T(8,128)(2,1)S(1)}, u32[]{:S(2)}, u32[]{:S(2)}) %collective-permute-start.16) | collective-permute-done | bytes 147488 | tf_op jit(solution)/shard_map/ppermute | solution.py:270
  311.3 18.3 %shard_map.194 = bf16[768,768]{1,0:T(8,128)(2,1)S(1)} custom-call(bf16[768,576]{1,0:T(8,128)(2,1)S(1)} %pad_maximum_fusion.4.a_ref, bf16[768,576]{1,0:T(8,128)(2,1)S(1)} %copy-done.1), custom_call_target="tpu_custom_call" | custom-call | flops 679477248 | bytes 23592960 | tf_op jit(solution)/shard_map/pallas_call | solution.py:250
  343.6 18.8 %shard_map.195 = bf16[768,768]{1,0:T(8,128)(2,1)S(1)} custom-call(bf16[768,768]{1,0:T(8,128)(2,1)S(1)} %get-tuple-element.142.a_ref, bf16[768,768]{1,0:T(8,128)(2,1)S(1)} %get-tuple-element.143.w_ref), custom_call_target="tpu_custom_call" | custom-call | flops 905969664 | bytes 23592960 | tf_op jit(solution)/shard_map/pallas_call | solution.py:250
  380.8 10.6 %shard_map.196 = (bf16[768,192]{1,0:T(8,128)(2,1)S(1)}, bf16[1536,192]{1,0:T(8,128)(2,1)S(1)}, bf16[1536,192]{1,0:T(8,128)(2,1)S(1)}) custom-call(bf16[768,192]{1,0:T(8,128)(2,1)S(1)} %copy-done.26, bf16[1536,192]{1,0:T(8,128)(2,1)S(1)} %copy-done.20, bf16[1536,192]{1,0:T(8,128)(2,1)S(1)} %copy-done.18, f32[1536,1]{1,0:T(8,128)S(1)} %copy-done.16, ...), custom_call_target="tpu_custom_call" | custom-call | flops 4529848320 | bytes 3538944 | tf_op jit(solution)/shard_map/pallas_call | solution.py:156
  405.0 19.8 %collective-permute-done.14 = bf16[384,576]{0,1:T(8,128)(2,1)S(1)} collective-permute-done((bf16[384,576]{0,1:T(8,128)(2,1)S(1)}, bf16[384,576]{0,1:T(8,128)(2,1)S(1)}, u32[]{:S(2)}, u32[]{:S(2)}) %collective-permute-start.14) | collective-permute-done | bytes 442400 | tf_op jit(solution)/shard_map/ppermute | solution.py:270
  432.9 6.9 %collective-permute-done.13 = bf16[384,576]{0,1:T(8,128)(2,1)S(1)} collective-permute-done((bf16[384,576]{0,1:T(8,128)(2,1)S(1)}, bf16[384,576]{0,1:T(8,128)(2,1)S(1)}, u32[]{:S(2)}, u32[]{:S(2)}) %collective-permute-start.13) | collective-permute-done | bytes 442400 | tf_op jit(solution)/shard_map/ppermute | solution.py:270
  443.3 18.3 %shard_map.197 = bf16[768,768]{1,0:T(8,128)(2,1)S(1)} custom-call(bf16[768,576]{1,0:T(8,128)(2,1)S(1)} %pad_maximum_fusion.5.a_ref, bf16[768,576]{1,0:T(8,128)(2,1)S(1)} %copy-done), custom_call_target="tpu_custom_call" | custom-call | flops 679477248 | bytes 23592960 | tf_op jit(solution)/shard_map/pallas_call | solution.py:250
  466.8 41.3 %all-reduce.2 = (f32[2,2,192]{2,1,0:T(2,128)}, f32[2,768]{1,0:T(2,128)}, f32[2,2,768]{2,1,0:T(2,128)}, f32[2,4,768]{2,1,0:T(4,128)}) all-reduce(f32[2,2,192]{2,1,0:T(2,128)} %pad_maximum_fusion.18, f32[2,768]{1,0:T(2,128)} %pad_maximum_fusion.17, ...), channel_id=1, replica_groups=mesh['dp'=4,'seq'=2,'head'=4] {'dp','seq'}, use_global_device_ids=true, to_apply=%region_20.21 | all-reduce | flops 11520 | bytes 92160 | tf_op jit(solution)/shard_map/psum | solution.py:426
  516.4 62.0 %all-reduce.6.cloned.1.call-done = (bf16[1,3,384,192]{2,3,1,0:T(8,128)(2,1)}, bf16[1,3,384,192]{2,3,1,0:T(8,128)(2,1)}, bf16[1,192,384]{2,1,0:T(8,128)(2,1)}, bf...) async-done(((bf16[1,3,384,192]{2,3,1,0:T(8,128)(2,1)}, ...) | async-done | bytes 3538960 | tf_op jit(solution)/shard_map/psum | solution.py:422
  (492 shorter events, 161.5 us)
Async XLA Ops:
  7.2 571.3 %all-reduce.6.cloned.1.call-start = ((), (), s32[]{:S(2)}) async-start(), calls=%async_computation | async-start | bytes 7077888 | tf_op jit(solution)/shard_map/psum | solution.py:422
  8.0 17.8 %collective-permute-start = (bf16[2,6,384]{2,1,0:T(8,128)(2,1)S(1)}, bf16[2,6,384]{2,1,0:T(8,128)(2,1)S(1)}, u32[]{:S(2)}, u32[]{:S(2)}) collective-permute-start(bf16[2,6,384]{2,1,0:T(8,128)(2,1)S(1)} %pad_maximum_fusion.15), channel_id=1, source_target_pairs={{0,4},{4,0},{1,5},{5,1},{2,6},{6,2},{3,7},{7,3},{8,12},{12,8},{9,1... | collective-permute-start | bytes 27656 | tf_op jit(solution)/shard_map/ppermute | solution.py:270
  13.2 31.2 %collective-permute-start.1 = (bf16[3,384,192]{1,2,0:T(8,128)(2,1)}, bf16[3,384,192]{1,2,0:T(8,128)(2,1)}, u32[]{:S(2)}, u32[]{:S(2)}) collective-permute-start(bf16[3,384,192]{1,2,0:T(8,128)(2,1)} %get-tuple-element.116), channel_id=1, source_target_pairs={{0,4},{4,0},{1,5},{5,1},{2,6},{6,2},{3,7},{7,3},{8,12},{12,8},{9,1... | collective-permute-start | bytes 1327112 | tf_op jit(solution)/shard_map/ppermute | solution.py:270
  13.2 33.2 %collective-permute-start.6 = (bf16[3,384,192]{1,2,0:T(8,128)(2,1)}, bf16[3,384,192]{1,2,0:T(8,128)(2,1)}, u32[]{:S(2)}, u32[]{:S(2)}) collective-permute-start(bf16[3,384,192]{1,2,0:T(8,128)(2,1)} %get-tuple-element.115), channel_id=1, source_target_pairs={{0,4},{4,0},{1,5},{5,1},{2,6},{6,2},{3,7},{7,3},{8,12},{12,8},{9,1... | collective-permute-start | bytes 1327112 | tf_op jit(solution)/shard_map/ppermute | solution.py:270
  17.0 22.3 %collective-permute-start.3 = (bf16[192,384]{1,0:T(8,128)(2,1)}, bf16[192,384]{1,0:T(8,128)(2,1)}, u32[]{:S(2)}, u32[]{:S(2)}) collective-permute-start(bf16[192,384]{1,0:T(8,128)(2,1)} %get-tuple-element.124), channel_id=1, source_target_pairs={{0,4},{4,0},{1,5},{5,1},{2,6},{6,2},{3,7},{7,3},{8,12},{12,8},{9,1... | collective-permute-start | bytes 442376 | tf_op jit(solution)/shard_map/ppermute | solution.py:270
  17.0 25.4 %collective-permute-start.8 = (bf16[192,384]{1,0:T(8,128)(2,1)}, bf16[192,384]{1,0:T(8,128)(2,1)}, u32[]{:S(2)}, u32[]{:S(2)}) collective-permute-start(bf16[192,384]{1,0:T(8,128)(2,1)} %get-tuple-element.123), channel_id=1, source_target_pairs={{0,4},{4,0},{1,5},{5,1},{2,6},{6,2},{3,7},{7,3},{8,12},{12,8},{9,1... | collective-permute-start | bytes 442376 | tf_op jit(solution)/shard_map/ppermute | solution.py:270
  25.9 68.7 %collective-permute-start.4 = (bf16[384,768]{1,0:T(8,128)(2,1)}, bf16[384,768]{1,0:T(8,128)(2,1)S(1)}, u32[]{:S(2)}, u32[]{:S(2)}) collective-permute-start(bf16[384,768]{1,0:T(8,128)(2,1)} %get-tuple-element.108), channel_id=1, source_target_pairs={{0,4},{4,0},{1,5},{5,1},{2,6},{6,2},{3,7},{7,3},{8,12},{12,8},{9,1... | collective-permute-start | bytes 1769480 | tf_op jit(solution)/shard_map/ppermute | solution.py:270
  27.3 134.0 %copy-start.107 = (f32[768]{0:T(1024)}, f32[768]{0:T(1024)S(1)}, u32[]{:S(2)}) copy-start(f32[768]{0:T(1024)S(1)} %get-tuple-element.50) | copy-start | bytes 9220
  39.3 55.3 %collective-permute-start.9 = (bf16[384,768]{1,0:T(8,128)(2,1)S(1)}, bf16[384,768]{1,0:T(8,128)(2,1)S(1)}, u32[]{:S(2)}, u32[]{:S(2)}) collective-permute-start(bf16[384,768]{1,0:T(8,128)(2,1)S(1)} %copy-done.89), channel_id=1, source_target_pairs={{0,4},{4,0},{1,5},{5,1},{2,6},{6,2},{3,7},{7,3},{8,12},{12,8},{9,1... | collective-permute-start | bytes 1769480 | tf_op jit(solution)/shard_map/ppermute | solution.py:270
  42.4 37.8 %collective-permute-start.10 = (bf16[768,384]{1,0:T(8,128)(2,1)S(1)}, bf16[768,384]{1,0:T(8,128)(2,1)S(1)}, u32[]{:S(2)}, u32[]{:S(2)}) collective-permute-start(bf16[768,384]{1,0:T(8,128)(2,1)S(1)} %copy-done.91), channel_id=1, source_target_pairs={{0,4},{4,0},{1,5},{5,1},{2,6},{6,2},{3,7},{7,3},{8,12},{12,8},{9,1... | collective-permute-start | bytes 1769480 | tf_op jit(solution)/shard_map/ppermute | solution.py:270
  44.4 48.5 %collective-permute-start.5 = (bf16[768,384]{1,0:T(8,128)(2,1)S(1)}, bf16[768,384]{1,0:T(8,128)(2,1)S(1)}, u32[]{:S(2)}, u32[]{:S(2)}) collective-permute-start(bf16[768,384]{1,0:T(8,128)(2,1)S(1)} %copy-done.90), channel_id=1, source_target_pairs={{0,4},{4,0},{1,5},{5,1},{2,6},{6,2},{3,7},{7,3},{8,12},{12,8},{9,1... | collective-permute-start | bytes 1769480 | tf_op jit(solution)/shard_map/ppermute | solution.py:270
  48.1 114.3 %copy-start.48 = (bf16[3,768,192]{1,2,0:T(8,128)(2,1)}, bf16[3,768,192]{1,2,0:T(8,128)(2,1)S(1)}, u32[]{:S(2)}) copy-start(bf16[3,768,192]{1,2,0:T(8,128)(2,1)S(1)} %get-tuple-element.148) | copy-start | bytes 2654212
  48.9 55.2 %collective-permute-start.2 = (bf16[768,384]{1,0:T(8,128)(2,1)S(1)}, bf16[768,384]{1,0:T(8,128)(2,1)S(1)}, u32[]{:S(2)}, u32[]{:S(2)}) collective-permute-start(bf16[768,384]{1,0:T(8,128)(2,1)S(1)} %fusion.49), channel_id=1, source_target_pairs={{0,4},{4,0},{1,5},{5,1},{2,6},{6,2},{3,7},{7,3},{8,12},{12,8},{9,1... | collective-permute-start | bytes 1769480 | tf_op jit(solution)/shard_map/ppermute | solution.py:270
  163.9 16.0 %collective-permute-start.7 = (bf16[768,384]{1,0:T(8,128)(2,1)}, bf16[768,384]{1,0:T(8,128)(2,1)}, u32[]{:S(2)}, u32[]{:S(2)}) collective-permute-start(bf16[768,384]{1,0:T(8,128)(2,1)} %fusion.50), channel_id=1, source_target_pairs={{0,4},{4,0},{1,5},{5,1},{2,6},{6,2},{3,7},{7,3},{8,12},{12,8},{9,1... | collective-permute-start | bytes 1769480 | tf_op jit(solution)/shard_map/ppermute | solution.py:270
  289.7 20.1 %collective-permute-start.11 = (bf16[768,384]{1,0:T(8,128)(2,1)S(1)}, bf16[768,384]{1,0:T(8,128)(2,1)S(1)}, u32[]{:S(2)}, u32[]{:S(2)}) collective-permute-start(bf16[768,384]{1,0:T(8,128)(2,1)S(1)} %pad_maximum_fusion.11), channel_id=1, source_target_pairs={{0,4},{4,0},{1,5},{5,1},{2,6},{6,2},{3,7},{7,3},{8,12},{12,8},{9,1... | collective-permute-start | bytes 1769480 | tf_op jit(solution)/shard_map/ppermute | solution.py:270
  290.3 18.8 %collective-permute-start.16 = (bf16[192,384]{1,0:T(8,128)(2,1)S(1)}, bf16[192,384]{1,0:T(8,128)(2,1)S(1)}, u32[]{:S(2)}, u32[]{:S(2)}) collective-permute-start(bf16[192,384]{1,0:T(8,128)(2,1)S(1)} %dynamic-slice_convert_fusion.6), channel_id=1, source_target_pairs={{0,4},{4,0},{1,5},{5,1},{2,6},{6,2},{3,7},{7,3},{8,12},{12,8},{9,1... | collective-permute-start | bytes 442376 | tf_op jit(solution)/shard_map/ppermute | solution.py:270
  294.0 98.9 %collective-permute-start.20 = (bf16[768,384]{1,0:T(8,128)(2,1)}, bf16[768,384]{1,0:T(8,128)(2,1)}, u32[]{:S(2)}, u32[]{:S(2)}) collective-permute-start(bf16[768,384]{1,0:T(8,128)(2,1)} %dynamic-slice_convert_fusion), channel_id=1, source_target_pairs={{0,4},{4,0},{1,5},{5,1},{2,6},{6,2},{3,7},{7,3},{8,12},{12,8},{9,1... | collective-permute-start | bytes 1769480 | tf_op jit(solution)/shard_map/ppermute | solution.py:270
  296.7 99.9 %collective-permute-start.18 = (bf16[384,768]{1,0:T(8,128)(2,1)}, bf16[384,768]{1,0:T(8,128)(2,1)}, u32[]{:S(2)}, u32[]{:S(2)}) collective-permute-start(bf16[384,768]{1,0:T(8,128)(2,1)} %dynamic-slice_convert_fusion.2), channel_id=1, source_target_pairs={{0,4},{4,0},{1,5},{5,1},{2,6},{6,2},{3,7},{7,3},{8,12},{12,8},{9,1... | collective-permute-start | bytes 1769480 | tf_op jit(solution)/shard_map/ppermute | solution.py:270
  371.1 57.6 %collective-permute-start.19 = (bf16[768,384]{1,0:T(8,128)(2,1)}, bf16[768,384]{1,0:T(8,128)(2,1)}, u32[]{:S(2)}, u32[]{:S(2)}) collective-permute-start(bf16[768,384]{1,0:T(8,128)(2,1)} %dynamic-slice_convert_fusion.1), channel_id=1, source_target_pairs={{0,4},{4,0},{1,5},{5,1},{2,6},{6,2},{3,7},{7,3},{8,12},{12,8},{9,1... | collective-permute-start | bytes 1769480 | tf_op jit(solution)/shard_map/ppermute | solution.py:270
  372.6 58.2 %collective-permute-start.17 = (bf16[384,768]{1,0:T(8,128)(2,1)}, bf16[384,768]{1,0:T(8,128)(2,1)}, u32[]{:S(2)}, u32[]{:S(2)}) collective-permute-start(bf16[384,768]{1,0:T(8,128)(2,1)} %dynamic-slice_convert_fusion.3), channel_id=1, source_target_pairs={{0,4},{4,0},{1,5},{5,1},{2,6},{6,2},{3,7},{7,3},{8,12},{12,8},{9,1... | collective-permute-start | bytes 1769480 | tf_op jit(solution)/shard_map/ppermute | solution.py:270
  374.8 28.7 %collective-permute-start.15 = (bf16[192,384]{1,0:T(8,128)(2,1)}, bf16[192,384]{1,0:T(8,128)(2,1)}, u32[]{:S(2)}, u32[]{:S(2)}) collective-permute-start(bf16[192,384]{1,0:T(8,128)(2,1)} %dynamic-slice_convert_fusion.7), channel_id=1, source_target_pairs={{0,4},{4,0},{1,5},{5,1},{2,6},{6,2},{3,7},{7,3},{8,12},{12,8},{9,1... | collective-permute-start | bytes 442376 | tf_op jit(solution)/shard_map/ppermute | solution.py:270
  393.0 32.8 %collective-permute-start.12 = (bf16[768,384]{1,0:T(8,128)(2,1)S(1)}, bf16[768,384]{1,0:T(8,128)(2,1)S(1)}, u32[]{:S(2)}, u32[]{:S(2)}) collective-permute-start(bf16[768,384]{1,0:T(8,128)(2,1)S(1)} %pad_maximum_fusion.10), channel_id=1, source_target_pairs={{0,4},{4,0},{1,5},{5,1},{2,6},{6,2},{3,7},{7,3},{8,12},{12,8},{9,1... | collective-permute-start | bytes 1769480 | tf_op jit(solution)/shard_map/ppermute | solution.py:270
  396.6 28.3 %collective-permute-start.14 = (bf16[384,576]{0,1:T(8,128)(2,1)S(1)}, bf16[384,576]{0,1:T(8,128)(2,1)S(1)}, u32[]{:S(2)}, u32[]{:S(2)}) collective-permute-start(bf16[384,576]{0,1:T(8,128)(2,1)S(1)} %dynamic-slice_convert_fusion.4), channel_id=1, source_target_pairs={{0,4},{4,0},{1,5},{5,1},{2,6},{6,2},{3,7},{7,3},{8,12},{12,8},{9,1... | collective-permute-start | bytes 1327112 | tf_op jit(solution)/shard_map/ppermute | solution.py:270
  428.1 11.7 %collective-permute-start.13 = (bf16[384,576]{0,1:T(8,128)(2,1)S(1)}, bf16[384,576]{0,1:T(8,128)(2,1)S(1)}, u32[]{:S(2)}, u32[]{:S(2)}) collective-permute-start(bf16[384,576]{0,1:T(8,128)(2,1)S(1)} %dynamic-slice_convert_fusion.5), channel_id=1, source_target_pairs={{0,4},{4,0},{1,5},{5,1},{2,6},{6,2},{3,7},{7,3},{8,12},{12,8},{9,1... | collective-permute-start | bytes 1327112 | tf_op jit(solution)/shard_map/ppermute | solution.py:270
  (157 other events, 1679.5 us)
Sparse Core Ops, SparseCore 0:
  440.9 137.5 all-reduce.5

commit v2 on v1

--- a/solution.py
+++ b/solution.py
@@ -104,9 +104,9 @@
 
 
 def attend_back_kernel(
-    heads, q_ref, k_ref, v_ref, bias_ref, lse_ref, o_ref, do_ref,
-    dq_ref, dk_ref, dv_ref, kt_ref, dk_sum, dv_sum,
+    heads, q_ref, k_ref, v_ref, bias_ref, lse_ref, o_ref, do_ref, dq_ref, *rest
 ):
+    *pair_refs, kt_ref, dk_sum, dv_sum = rest
     step = pl.program_id(0)
 
     @pl.when(step == 0)
@@ -142,18 +142,26 @@
 
     @pl.when(step == pl.num_programs(0) - 1)
     def _():
-        dk_ref[...] = dk_sum[...].astype(jnp.bfloat16)
-        dv_ref[...] = dv_sum[...].astype(jnp.bfloat16)
-
-
-def attend_back(queries, key_all, value_all, bias, logsum, attended, d_attended):
+        rows = pair_refs[0].shape[0]
+        me = lax.axis_index("seq")
+        starts = (me * rows, (1 - me) * rows) if len(pair_refs) == 2 else (0,)
+        for start, pair_ref in zip(starts, pair_refs):
+            place = pl.ds(pl.multiple_of(start, 16), rows)
+            pair_ref[...] = jnp.concatenate(
+                [dk_sum[place, :], dv_sum[place, :]], axis=1
+            ).astype(jnp.bfloat16)
+
+
+def attend_back(queries, key_all, value_all, bias, logsum, attended, d_attended, parts):
     rows, width = queries.shape
     keys = key_all.shape[0]
     heads = width // HD
     block = row_block(rows)
     row_spec = pl.BlockSpec((block, width), lambda i: (i, 0))
     key_spec = pl.BlockSpec((keys, width), lambda i: (0, 0))
-    return pl.pallas_call(
+    pieces = 2 if parts == 2 else 1
+    pair = (keys // pieces, 2 * width)
+    d_query, *d_pairs = pl.pallas_call(
         functools.partial(attend_back_kernel, heads),
         grid=(rows // block,),
         in_specs=[
@@ -165,12 +173,9 @@
             row_spec,
             row_spec,
         ],
-        out_specs=[row_spec, key_spec, key_spec],
-        out_shape=[
-            jax.ShapeDtypeStruct((rows, width), jnp.bfloat16),
-            jax.ShapeDtypeStruct((keys, width), jnp.bfloat16),
-            jax.ShapeDtypeStruct((keys, width), jnp.bfloat16),
-        ],
+        out_specs=[row_spec] + [pl.BlockSpec(pair, lambda i: (0, 0))] * pieces,
+        out_shape=[jax.ShapeDtypeStruct((rows, width), jnp.bfloat16)]
+        + [jax.ShapeDtypeStruct(pair, jnp.bfloat16)] * pieces,
         scratch_shapes=[
             pltpu.VMEM((width, keys), jnp.bfloat16),
             pltpu.VMEM((keys, width), jnp.float32),
@@ -181,6 +186,7 @@
             flops=20 * rows * keys * width, bytes_accessed=12 * keys * width, transcendentals=rows * keys * heads
         ),
     )(queries, key_all, value_all, bias, logsum, attended, d_attended)
+    return (d_query, d_pairs)
 
 
 def head_sum_kernel(dims, chunks, a_ref, w_ref, out_ref, first, landed, own, chip, crossed, last, done, send, recv):
@@ -280,21 +286,70 @@
     )
 
 
-def scatter_seq(values, axis):
+def after(earlier, *values):
+    return lax.optimization_barrier((earlier, *values))[1:]
+
+
+def scatter_seq(values):
     if lax.axis_size("seq") != 2:
-        return lax.psum_scatter(
-            values.astype(jnp.bfloat16), "seq", scatter_dimension=axis, tiled=True
-        )
-    size = values.shape[axis] // 2
+        return (None, values.astype(jnp.bfloat16))
+    size = values.shape[1] // 2
     me = lax.axis_index("seq")
-    kept = lax.dynamic_slice_in_dim(values, me * size, size, axis)
-    sent = lax.dynamic_slice_in_dim(values, (1 - me) * size, size, axis)
-    return (kept + swap(sent.astype(jnp.bfloat16)).astype(jnp.float32)).astype(jnp.bfloat16)
+    kept = lax.dynamic_slice_in_dim(values, me * size, size, 1)
+    sent = lax.dynamic_slice_in_dim(values, (1 - me) * size, size, 1)
+    return (kept, sent.astype(jnp.bfloat16))
+
+
+def finish_seq(kept, sent):
+    if lax.axis_size("seq") != 2:
+        return lax.psum_scatter(sent, "seq", scatter_dimension=1, tiled=True)
+    return (kept.astype(jnp.float32) + swap(sent).astype(jnp.float32)).astype(jnp.bfloat16)
+
+
+def shifted(values, axis, shift):
+    n = lax.axis_size(axis)
+    return lax.ppermute(values, axis, [(i, (i + shift) % n) for i in range(n)])
+
+
+def sum_dp(values):
+    n = lax.axis_size("dp")
+    me = lax.axis_index("dp")
+    size = values.shape[0] // n
+
+    def share(shift):
+        return lax.dynamic_slice_in_dim(values, (me + shift) % n * size, size, 0)
+
+    total = share(0).astype(jnp.float32)
+    for shift in range(1, n):
+        total = total + shifted(share(shift), "dp", shift).astype(jnp.float32)
+    total = total.astype(jnp.bfloat16)
+    result = jnp.zeros(values.shape, jnp.bfloat16)
+    result = lax.dynamic_update_slice_in_dim(result, total, me * size, 0)
+    for shift in range(1, n):
+        result = lax.dynamic_update_slice_in_dim(
+            result, shifted(total, "dp", shift), (me + n - shift) % n * size, 0
+        )
+    return result
+
+
+def sum_pairwise(values, axis):
+    n = lax.axis_size(axis)
+    step = 1
+    while step < n:
+        values = values + lax.ppermute(values, axis, [(i, i ^ step) for i in range(n)])
+        step *= 2
+    return values
 
 
 def own_part(values):
     size = values.shape[-1] // lax.axis_size("seq")
     return lax.dynamic_slice_in_dim(values, lax.axis_index("seq") * size, size, values.ndim - 1)
+
+
+def cross(left, right):
+    return lax.dot_general(
+        left, right, (((0,), (0,)), ((), ())), preferred_element_type=jnp.float32
+    )
 
 
 def on_device(
@@ -304,49 +359,48 @@
     row_count = clip_count * rows_dev
     layers = w_qkv.shape[0]
     head_width = w_qkv.shape[3]
+    units = w_up.shape[2]
     query_scale = HD ** (-0.5)
     parts = lax.axis_size("seq")
-    me = lax.axis_index("seq")
     key_length = rows_dev * parts
     positions = jnp.arange(key_length, dtype=jnp.int32)
-    if parts == 2:
-        positions = (positions + me * rows_dev) % key_length
     bias = jnp.where(positions < lengths[0], 0.0, -1e30).astype(jnp.float32)[:, None]
 
-    vectors = gather_seq(jnp.concatenate([gains, shifts], axis=1), 2).astype(jnp.float32)
+    vectors = jnp.concatenate([gains, shifts], axis=1)
+    vectors = lax.all_gather(vectors, "seq", axis=2, tiled=True).astype(jnp.float32)
     gain_all, shift_all = vectors[:, :2], vectors[:, 2:]
-    weights = []
-    for l in range(layers):
-        qkv = gather_seq(w_qkv[l], 1)
-        weights.append(
-            (
-                qkv.transpose(1, 0, 2).reshape(model_width, 3 * head_width),
-                gather_seq(w_out[l], 1),
-                gather_seq(w_up[l], 0),
-                gather_seq(w_down[l], 1),
-            )
-        )
+    flat_qkv = w_qkv.transpose(0, 2, 1, 3).reshape(layers, -1, 3 * head_width)
+    qkv_full = lax.all_gather(flat_qkv[0], "seq", axis=0, tiled=True)
 
     stream = frames.astype(jnp.float32).reshape(row_count, model_width)
     saved_layers = []
+    weights = []
+    next_weights = None
     for l in range(layers):
-        qkv_full, out_full, up_full, down_full = weights[l]
         gain_pair, shift_set = gain_all[l], shift_all[l]
         bias_pair = qv_bias[l].astype(jnp.float32)
+        if l > 0:
+            qkv_full, out_full, up_full, down_full = next_weights
         normed = normalize(stream, gain_pair[0], shift_set[0]).astype(jnp.bfloat16)
         pair = jnp.dot(normed, qkv_full[:, head_width:], preferred_element_type=jnp.float32)
         pair = pair + jnp.concatenate([jnp.zeros_like(bias_pair[1]), bias_pair[1]])
-        pair = pair.astype(jnp.bfloat16)
-        if parts == 2:
-            pair_all = jnp.concatenate([pair, swap(pair)], axis=0)
-        else:
-            pair_all = lax.all_gather(pair, "seq", axis=0, tiled=True)
+        pair_all = lax.all_gather(pair.astype(jnp.bfloat16), "seq", axis=0, tiled=True)
+        if l == 0:
+            own = after(pair_all, w_out[0], w_up[0], w_down[0])
+            out_full = gather_seq(own[0], 1)
+            own = after(out_full, own[1])
+            up_full = gather_seq(own[0], 0)
+            down_full = gather_seq(after(up_full, w_down[0])[0], 1)
         key_all, value_all = pair_all[:, :head_width], pair_all[:, head_width:]
         queries = jnp.dot(normed, qkv_full[:, :head_width], preferred_element_type=jnp.float32)
         queries = ((queries + bias_pair[0]) * query_scale).astype(jnp.bfloat16)
         attended, logsum = attend(queries, key_all, value_all, bias)
         mid = stream + head_sum(attended, out_full, False, 1).astype(jnp.float32) + shift_set[1]
         normed_two = normalize(mid, gain_pair[1], shift_set[2]).astype(jnp.bfloat16)
+        weights.append((qkv_full, out_full, up_full, down_full))
+        if l + 1 < layers:
+            own = after(normed_two, flat_qkv[l + 1], w_out[l + 1], w_up[l + 1], w_down[l + 1])
+            next_weights = tuple(gather_seq(w, axis) for w, axis in zip(own, (0, 1, 0, 1)))
         hidden_pre = jnp.dot(normed_two, up_full, preferred_element_type=jnp.float32) + up_bias[
             l
         ].astype(jnp.float32)
@@ -375,13 +429,12 @@
         gelu_value, gelu_pull = jax.vjp(gelu_exact, hidden_pre)
         d_hidden = gelu_pull(d_act)[0].astype(jnp.bfloat16)
         d_up_bias = column_sum(d_hidden)
+        kept, sent = scatter_seq(
+            jnp.concatenate([cross(activated, grad_low), cross(d_hidden, normed_two)], axis=0)
+        )
+        d_hidden, sent = lax.optimization_barrier((d_hidden, sent))
+        share_mlp = finish_seq(kept, sent)
         d_norm_two = head_sum(d_hidden, up_full, True, 3).astype(jnp.float32)
-        share_down = scatter_seq(
-            jnp.dot(activated.T, grad_low, preferred_element_type=jnp.float32), 1
-        )
-        share_up = scatter_seq(
-            jnp.dot(normed_two.T, d_hidden, preferred_element_type=jnp.float32), 0
-        )
         norm_value, norm_pull = jax.vjp(normalize, mid, gain_pair[1], shift_set[2])
         d_mid, d_gain_two, d_shift_two = norm_pull(d_norm_two)
         grad_stream = grad_stream + d_mid
@@ -390,42 +443,47 @@
         d_attended = jnp.dot(grad_low, out_full.T, preferred_element_type=jnp.float32).astype(
             jnp.bfloat16
         )
-        d_query, d_key_part, d_value_part = attend_back(
-            queries, key_all, value_all, bias, logsum, attended, d_attended
-        )
-        d_pair = jnp.concatenate([d_key_part, d_value_part], axis=1)
+        d_query, d_pairs = attend_back(
+            queries, key_all, value_all, bias, logsum, attended, d_attended, parts
+        )
         if parts == 2:
             d_pair = (
-                d_pair[:rows_dev].astype(jnp.float32) + swap(d_pair[rows_dev:]).astype(jnp.float32)
+                d_pairs[0].astype(jnp.float32) + swap(d_pairs[1]).astype(jnp.float32)
             ).astype(jnp.bfloat16)
         else:
-            d_pair = lax.psum_scatter(d_pair, "seq", scatter_dimension=0, tiled=True)
-        share_out = scatter_seq(
-            jnp.dot(attended.T, grad_low, preferred_element_type=jnp.float32), 1
-        )
+            d_pair = lax.psum_scatter(d_pairs[0], "seq", scatter_dimension=0, tiled=True)
         d_qkv = jnp.concatenate([d_query, d_pair], axis=1)
+        kept, sent = scatter_seq(
+            jnp.concatenate([cross(d_qkv, normed), cross(attended, grad_low)], axis=0)
+        )
+        d_qkv, sent = lax.optimization_barrier((d_qkv, sent))
+        share_attn = finish_seq(kept, sent)
         d_normed = head_sum(d_qkv, qkv_full, True, 4).astype(jnp.float32)
-        d_qkv_weight = jnp.dot(normed.T, d_qkv, preferred_element_type=jnp.float32)
-        share_qkv = scatter_seq(d_qkv_weight, 0)
-        share_qkv = share_qkv.reshape(-1, 3, head_width).transpose(1, 0, 2)
         d_bias = column_sum(d_qkv)
         norm_value, norm_pull = jax.vjp(normalize, stream_in, gain_pair[0], shift_set[0])
         d_before, d_gain_one, d_shift_one = norm_pull(d_normed)
         grad_stream = grad_stream + d_before
-        owned[l] = (share_qkv, share_out, share_up, share_down)
-        small[l] = (
-            jnp.stack([d_bias[:head_width], d_bias[2 * head_width :]]),
-            d_up_bias,
-            jnp.stack([d_gain_one, d_gain_two]),
-            jnp.stack([d_shift_one, d_shift_attn, d_shift_two, d_shift_mlp]),
-        )
-    owned = lax.psum(owned, "dp")
-    grad_qkv, grad_out_weight, grad_up_weight, grad_down_weight = (
-        stack_member(owned, p).astype(jnp.float32) for p in range(4)
+        owned[l] = (sum_dp(share_mlp), sum_dp(share_attn))
+        small[l] = [
+            d_gain_one, d_gain_two, d_shift_one, d_shift_attn, d_shift_two, d_shift_mlp,
+            d_up_bias, d_bias[:head_width], d_bias[2 * head_width :],
+        ]
+    vector_sums = jnp.concatenate([v for entry in small for v in entry]).reshape(-1, 128)
+    vector_sums = sum_pairwise(sum_pairwise(vector_sums, "seq"), "dp").reshape(layers, -1)
+    d = model_width
+    grad_gain_set = vector_sums[:, : 2 * d].reshape(layers, 2, d)
+    grad_shift_set = vector_sums[:, 2 * d : 6 * d].reshape(layers, 4, d)
+    grad_bias_up = vector_sums[:, 6 * d : 6 * d + units]
+    grad_bias_pair = vector_sums[:, 6 * d + units :].reshape(layers, 2, head_width)
+
+    mlp = [entry[0].astype(jnp.float32) for entry in owned]
+    attn = [entry[1].astype(jnp.float32) for entry in owned]
+    grad_down_weight = jnp.stack([m[:units] for m in mlp])
+    grad_up_weight = jnp.stack([m[units:].T for m in mlp])
+    grad_qkv = jnp.stack(
+        [m[: 3 * head_width].reshape(3, head_width, -1).transpose(0, 2, 1) for m in attn]
     )
-    grad_bias_pair, grad_bias_up, grad_gain_set, grad_shift_set = lax.psum(
-        tuple(stack_member(small, p) for p in range(4)), ("dp", "seq")
-    )
+    grad_out_weight = jnp.stack([m[3 * head_width :] for m in attn])
     grad_frames = grad_stream.reshape(clip_count, rows_dev, model_width)
     return (
         output,

time: 598 us -> 655 us (1.095)
  starting transfers between devices: 19.9 us -> 59.9 us
  waiting for transfers between devices: 175 us -> 204 us
  blocking collectives: 41.3 us -> 18.1 us
  local copies, waits for them, and re-layouts: 45.5 us -> 57.2 us
    ppermute x0 -> x27, waiting for transfers between devices: none -> 98 us  [the longest x24 91.5 us: shifted(): return lax.ppermute(values, axis, [(i, (i + shift) % n) for i in range(n)])]
    psum x1 -> x0, waiting for transfers between devices: 62 us -> none  [on_device(): owned = lax.psum(owned, 'dp')]
    ppermute x0 -> x27, starting transfers between devices: none -> 46.5 us  [the longest x24 43.8 us: shifted(): return lax.ppermute(values, axis, [(i, (i + shift) % n) for i in range(n)])]
    ppermute x21 -> x13, waiting for transfers between devices: 113 us -> 71.4 us  [swap(): return lax.ppermute(values, 'seq', [(0, 1), (1, 0)])]
    psum x1 -> x0, blocking collectives: 41.3 us -> none  [on_device(): lax.psum(tuple((stack_member(small, p) for p in range(4))), ('dp', 'seq'))]
    all_gather x0 -> x2, waiting for transfers between devices: none -> 34.8 us  [on_device(): lax.all_gather(pair.astype(jnp.bfloat16), 'seq', axis=0, tiled=True)]
    all_gather x0 -> x2, blocking collectives: none -> 18.1 us  [the longest x1 12.8 us: on_device(): qkv_full = lax.all_gather(flat_qkv[0], 'seq', axis=0, tiled=True)]
    unnamed x318 -> x305, local copies, waits for them, and re-layouts: 19.8 us -> 29 us
  transfers between devices with their start and end apart: 22 -> 42, of which waited for: 11 -> 22; matrix products, arithmetic and copies ran while one was open for 14% -> 14% of each run, Pallas kernels for 11% -> 15%
where the time goes in v2:
time: 655 us; the launch traced here: 648 us
  waiting for transfers between devices  204 us (31%)
  Pallas kernels  190 us (29%)
  other arithmetic  65.6 us (10%)
  starting transfers between devices  59.9 us (9%)
  local copies, waits for them, and re-layouts  57.2 us (9%)
  matrix products  35.4 us (5%)
  blocking collectives  18.1 us (3%)
  between operations  16.9 us (3%)
    pallas_call x8, Pallas kernels, head_sum(): pl.pallas_call(functools.partial(head_sum_kernel, NT if transposed else N...  147 us
    ppermute x24, waiting for transfers between devices, shifted(): return lax.ppermute(values, axis, [(i, (i + shift) % n) for i in range(n)])  91.5 us
    ppermute x13, waiting for transfers between devices, swap(): return lax.ppermute(values, 'seq', [(0, 1), (1, 0)])  71.4 us
    ppermute x24, starting transfers between devices, shifted(): return lax.ppermute(values, axis, [(i, (i + shift) % n) for i in range(n)])  43.8 us
    all_gather x2, waiting for transfers between devices, on_device(): lax.all_gather(pair.astype(jnp.bfloat16), 'seq', axis=0, tiled=True)  34.8 us
    unnamed x305, local copies, waits for them, and re-layouts  29 us
    pallas_call x2, Pallas kernels, attend_back(): pl.pallas_call(functools.partial(attend_back_kernel, heads), grid=(rows /...  23.4 us
    pallas_call x2, Pallas kernels, attend(): pl.pallas_call(functools.partial(attend_kernel, heads), grid=(rows // blo...  19.6 us
  transfers between devices with their start and end apart: 42, of which 22 were waited for; matrix products, arithmetic and copies ran while one was open for 14% of the time, Pallas kernels for 15%

profile of v2, /device:TPU:0, one launch (start us, length us, event | category | flops | bytes accessed | tf_op | source)
XLA Modules:
  0.0 647.6 jit_solution(10826485234682266751)
XLA Ops:
  18.5 12.8 %all_gather.13.w_ref = bf16[768,576]{1,0:T(8,128)(2,1)S(1)} all-gather(bf16[384,576]{1,0:T(8,128)(2,1)S(1)} %copy.37), channel_id=1, replica_groups=mesh['dp'=4,'seq'=2,'head'=4] {'seq'}, dimensions={0}, use_global_device_ids=true | all-gather | bytes 1327104 | tf_op jit(solution)/shard_map/all_gather | solution.py:373
  41.3 17.0 %all-gather.3.cloned.1.call-done = bf16[1536,384]{1,0:T(8,128)(2,1)} async-done(((bf16[768,384]{1,0:T(8,128)(2,1)}), bf16[1536,384]{1,0:T(8,128)(2,1)}) %all-gather.3.cloned.1.call-update) | async-done | bytes 1179664 | tf_op jit(solution)/shard_map/all_gather | solution.py:387
  60.4 9.8 %shard_map.186 = (bf16[768,192]{1,0:T(8,128)(2,1)S(1)}, f32[3,3,256]{2,1,0:T(4,128)S(1)}) custom-call(bf16[768,192]{1,0:T(8,128)(2,1)S(1)} %fusion.63.q_ref, bf16[1536,192]{1,0:T(8,128)(2,1)S(1)} %get-tuple-element.172.k_ref, bf16[1536,192]{1,0:T(8,128)(2,1)S(1)} %get-tuple-element.171.v_ref, f32[1536,1]{1,0:T(8,128)S(1)} %fusion.79.bias_ref), custom_call_target="tpu_custom_call" | custom-call | flops 1811939328 | bytes 1769472 | tf_op jit(solution)/shard_map/pallas_call | solution.py:81
  71.1 18.3 %shard_map.187 = bf16[768,768]{1,0:T(8,128)(2,1)S(1)} custom-call(bf16[768,192]{1,0:T(8,128)(2,1)S(1)} %get-tuple-element.36.a_ref.o_ref, bf16[192,768]{1,0:T(8,128)(2,1)S(1)} %pad_maximum_fusion.11.w_ref), custom_call_target="tpu_custom_call" | custom-call | flops 226492416 | bytes 23592960 | tf_op jit(solution)/shard_map/pallas_call | solution.py:256
  134.6 27.3 %collective-permute-done.2 = bf16[768,384]{1,0:T(8,128)(2,1)S(1)} collective-permute-done((bf16[768,384]{1,0:T(8,128)(2,1)S(1)}, bf16[768,384]{1,0:T(8,128)(2,1)S(1)}, u32[]{:S(2)}, u32[]{:S(2)}) %collective-permute-start.2) | collective-permute-done | bytes 589856 | tf_op jit(solution)/shard_map/ppermute | solution.py:276
  163.0 18.3 %shard_map.188 = bf16[768,768]{1,0:T(8,128)(2,1)S(1)} custom-call(bf16[768,768]{1,0:T(8,128)(2,1)S(1)} %get-tuple-element.143.a_ref, bf16[768,768]{1,0:T(8,128)(2,1)S(1)} %pad_maximum_fusion.5.w_ref), custom_call_target="tpu_custom_call" | custom-call | flops 905969664 | bytes 23592960 | tf_op jit(solution)/shard_map/pallas_call | solution.py:256
  192.3 17.8 %all-gather.5.cloned.1.call-done = bf16[1536,384]{1,0:T(8,128)(2,1)} async-done(((bf16[768,384]{1,0:T(8,128)(2,1)}), bf16[1536,384]{1,0:T(8,128)(2,1)}) %all-gather.5.cloned.1.call-update) | async-done | bytes 1179664 | tf_op jit(solution)/shard_map/all_gather | solution.py:387
  212.0 9.8 %shard_map.189 = (bf16[768,192]{1,0:T(8,128)(2,1)S(1)}, f32[3,3,256]{2,1,0:T(4,128)S(1)}) custom-call(bf16[768,192]{1,0:T(8,128)(2,1)S(1)} %copy-done.28, bf16[1536,192]{1,0:T(8,128)(2,1)S(1)} %get-tuple-element.162.k_ref, bf16[1536,192]{1,0:T(8,128)(2,1)S(1)} %get-tuple-element.161.v_ref, f32[1536,1]{1,0:T(8,128)S(1)} %copy-done.11), custom_call_target="tpu_custom_call" | custom-call | flops 1811939328 | bytes 1769472 | tf_op jit(solution)/shard_map/pallas_call | solution.py:81
  221.8 18.3 %shard_map.190 = bf16[768,768]{1,0:T(8,128)(2,1)S(1)} custom-call(bf16[768,192]{1,0:T(8,128)(2,1)S(1)} %get-tuple-element.42.a_ref.o_ref, bf16[192,768]{1,0:T(8,128)(2,1)S(1)} %copy-done.9), custom_call_target="tpu_custom_call" | custom-call | flops 226492416 | bytes 23592960 | tf_op jit(solution)/shard_map/pallas_call | solution.py:256
  249.9 18.3 %shard_map.191 = bf16[768,768]{1,0:T(8,128)(2,1)S(1)} custom-call(bf16[768,768]{1,0:T(8,128)(2,1)S(1)} %get-tuple-element.137.a_ref, bf16[768,768]{1,0:T(8,128)(2,1)S(1)} %pad_maximum_fusion.7.w_ref), custom_call_target="tpu_custom_call" | custom-call | flops 905969664 | bytes 23592960 | tf_op jit(solution)/shard_map/pallas_call | solution.py:256
  277.4 19.0 %shard_map.192 = bf16[768,768]{1,0:T(8,128)(2,1)S(1)} custom-call(bf16[768,768]{1,0:T(8,128)(2,1)S(1)} %get-tuple-element.46.a_ref, bf16[768,768]{1,0:T(8,128)(2,1)S(1)} %pad_maximum_fusion.6.w_ref), custom_call_target="tpu_custom_call" | custom-call | flops 905969664 | bytes 23592960 | tf_op jit(solution)/shard_map/pallas_call | solution.py:256
  307.2 12.0 %shard_map.193 = (bf16[768,192]{1,0:T(8,128)(2,1)S(1)}, bf16[768,384]{1,0:T(8,128)(2,1)S(1)}, bf16[768,384]{1,0:T(8,128)(2,1)}) custom-call(bf16[768,192]{1,0:T(8,128)(2,1)S(1)} %copy-done.29, bf16[1536,192]{1,0:T(8,128)(2,1)S(1)} %copy-done.21, bf16[1536,192]{1,0:T(8,128)(2,1)S(1)} %copy-done.19, f32[1536,1]{1,0:T(8,128)S(1)} %copy-done.12, ...), custom_call_target="tpu_custom_call" | custom-call | flops 4529848320 | bytes 3538944 | tf_op jit(solution)/shard_map/pallas_call | solution.py:164
  324.6 12.6 %collective-permute-done.7 = bf16[768,384]{1,0:T(8,128)(2,1)} collective-permute-done((bf16[768,384]{1,0:T(8,128)(2,1)}, bf16[768,384]{1,0:T(8,128)(2,1)}, u32[]{:S(2)}, u32[]{:S(2)}) %collective-permute-start.7) | collective-permute-done | bytes 589856 | tf_op jit(solution)/shard_map/ppermute | solution.py:276
  341.8 18.3 %shard_map.194 = bf16[768,768]{1,0:T(8,128)(2,1)S(1)} custom-call(bf16[768,576]{1,0:T(8,128)(2,1)S(1)} %pad_maximum_fusion.8.a_ref, bf16[768,576]{1,0:T(8,128)(2,1)S(1)} %pad_maximum_fusion.3.w_ref), custom_call_target="tpu_custom_call" | custom-call | flops 679477248 | bytes 23592960 | tf_op jit(solution)/shard_map/pallas_call | solution.py:256
  375.8 18.6 %shard_map.195 = bf16[768,768]{1,0:T(8,128)(2,1)S(1)} custom-call(bf16[768,768]{1,0:T(8,128)(2,1)S(1)} %get-tuple-element.52.a_ref, bf16[768,768]{1,0:T(8,128)(2,1)S(1)} %copy-done), custom_call_target="tpu_custom_call" | custom-call | flops 905969664 | bytes 23592960 | tf_op jit(solution)/shard_map/pallas_call | solution.py:256
  411.2 11.4 %shard_map.196 = (bf16[768,192]{1,0:T(8,128)(2,1)S(1)}, bf16[768,384]{1,0:T(8,128)(2,1)S(1)}, bf16[768,384]{1,0:T(8,128)(2,1)S(1)}) custom-call(bf16[768,192]{1,0:T(8,128)(2,1)S(1)} %copy-done.31, bf16[1536,192]{1,0:T(8,128)(2,1)S(1)} %copy-done.17, bf16[1536,192]{1,0:T(8,128)(2,1)S(1)} %copy-done.15, f32[1536,1]{1,0:T(8,128)S(1)} %copy-done.13, ...), custom_call_target="tpu_custom_call" | custom-call | flops 4529848320 | bytes 3538944 | tf_op jit(solution)/shard_map/pallas_call | solution.py:164
  425.9 12.9 %collective-permute-done.8 = bf16[768,384]{1,0:T(8,128)(2,1)S(1)} collective-permute-done((bf16[768,384]{1,0:T(8,128)(2,1)S(1)}, bf16[768,384]{1,0:T(8,128)(2,1)S(1)}, u32[]{:S(2)}, u32[]{:S(2)}) %collective-permute-start.8) | collective-permute-done | bytes 589856 | tf_op jit(solution)/shard_map/ppermute | solution.py:276
  442.4 18.3 %shard_map.197 = bf16[768,768]{1,0:T(8,128)(2,1)S(1)} custom-call(bf16[768,576]{1,0:T(8,128)(2,1)S(1)} %pad_maximum_fusion.9.a_ref, bf16[768,576]{1,0:T(8,128)(2,1)S(1)} %copy-done.2), custom_call_target="tpu_custom_call" | custom-call | flops 679477248 | bytes 23592960 | tf_op jit(solution)/shard_map/pallas_call | solution.py:256
  514.3 11.0 %collective-permute-done.35 = bf16[384,384]{1,0:T(8,128)(2,1)S(1)} collective-permute-done((bf16[384,384]{1,0:T(8,128)(2,1)}, bf16[384,384]{1,0:T(8,128)(2,1)S(1)}, u32[]{:S(2)}, u32[]{:S(2)}) %collective-permute-start.35) | collective-permute-done | bytes 294944 | tf_op jit(solution)/shard_map/ppermute | solution.py:311
  543.1 12.6 %collective-permute-done.38 = bf16[384,384]{1,0:T(8,128)(2,1)S(1)} collective-permute-done((bf16[384,384]{1,0:T(8,128)(2,1)S(1)}, bf16[384,384]{1,0:T(8,128)(2,1)S(1)}, u32[]{:S(2)}, u32[]{:S(2)}) %collective-permute-start.38) | collective-permute-done | bytes 294944 | tf_op jit(solution)/shard_map/ppermute | solution.py:311
  555.7 10.6 %collective-permute-start.27 = (bf16[384,384]{1,0:T(8,128)(2,1)S(1)}, bf16[384,384]{1,0:T(8,128)(2,1)S(1)}, u32[]{:S(2)}, u32[]{:S(2)}) collective-permute-start(bf16[384,384]{1,0:T(8,128)(2,1)S(1)} %get-tuple-element.150), channel_id=1, source_target_pairs={{0,8},{8,16},{16,24},{24,0},{1,9},{9,17},{17,25},{25,1},{2,10},{10... | collective-permute-start | bytes 884744 | tf_op jit(solution)/shard_map/ppermute | solution.py:311
  570.1 12.0 %collective-permute-done.11 = bf16[192,384]{1,0:T(8,128)(2,1)S(1)} collective-permute-done((bf16[192,384]{1,0:T(8,128)(2,1)S(1)}, bf16[192,384]{1,0:T(8,128)(2,1)S(1)}, u32[]{:S(2)}, u32[]{:S(2)}) %collective-permute-start.11) | collective-permute-done | bytes 147488 | tf_op jit(solution)/shard_map/ppermute | solution.py:311
  592.5 15.5 %collective-permute-done.14 = bf16[192,384]{1,0:T(8,128)(2,1)S(1)} collective-permute-done((bf16[192,384]{1,0:T(8,128)(2,1)S(1)}, bf16[192,384]{1,0:T(8,128)(2,1)S(1)}, u32[]{:S(2)}, u32[]{:S(2)}) %collective-permute-start.14) | collective-permute-done | bytes 147488 | tf_op jit(solution)/shard_map/ppermute | solution.py:311
  623.5 10.6 %collective-permute-done.31 = bf16[384,384]{1,0:T(8,128)(2,1)S(1)} collective-permute-done((bf16[384,384]{1,0:T(8,128)(2,1)S(1)}, bf16[384,384]{1,0:T(8,128)(2,1)S(1)}, u32[]{:S(2)}, u32[]{:S(2)}) %collective-permute-start.31) | collective-permute-done | bytes 294944 | tf_op jit(solution)/shard_map/ppermute | solution.py:311
  (538 shorter events, 267.6 us)
Async XLA Ops:
  7.2 51.1 %all-gather.3.cloned.1.call-start = ((), (), s32[]{:S(2)}) async-start(), calls=%async_computation | async-start | bytes 1769472 | tf_op jit(solution)/shard_map/all_gather | solution.py:387
  33.9 176.2 %all-gather.5.cloned.1.call-start = ((), (), s32[]{:S(2)}) async-start(), calls=%async_computation.1 | async-start | bytes 1769472 | tf_op jit(solution)/shard_map/all_gather | solution.py:387
  94.3 19.2 %collective-permute-start.3 = (bf16[384,576]{1,0:T(8,128)(2,1)}, bf16[384,576]{1,0:T(8,128)(2,1)}, u32[]{:S(2)}, u32[]{:S(2)}) collective-permute-start(bf16[384,576]{1,0:T(8,128)(2,1)} %copy.40), channel_id=1, source_target_pairs={{0,4},{4,0},{1,5},{5,1},{2,6},{6,2},{3,7},{7,3},{8,12},{12,8},{9,1... | collective-permute-start | bytes 1327112 | tf_op jit(solution)/shard_map/ppermute | solution.py:276
  97.6 26.7 %collective-permute-start.1 = (bf16[384,768]{1,0:T(8,128)(2,1)S(1)}, bf16[384,768]{1,0:T(8,128)(2,1)S(1)}, u32[]{:S(2)}, u32[]{:S(2)}) collective-permute-start(bf16[384,768]{1,0:T(8,128)(2,1)S(1)} %copy-done.72), channel_id=1, source_target_pairs={{0,4},{4,0},{1,5},{5,1},{2,6},{6,2},{3,7},{7,3},{8,12},{12,8},{9,1... | collective-permute-start | bytes 1769480 | tf_op jit(solution)/shard_map/ppermute | solution.py:276
  100.7 86.2 %collective-permute-start.6 = (bf16[768,384]{1,0:T(8,128)(2,1)S(1)}, bf16[768,384]{1,0:T(8,128)(2,1)}, u32[]{:S(2)}, u32[]{:S(2)}) collective-permute-start(bf16[768,384]{1,0:T(8,128)(2,1)S(1)} %copy-done.70), channel_id=1, source_target_pairs={{0,4},{4,0},{1,5},{5,1},{2,6},{6,2},{3,7},{7,3},{8,12},{12,8},{9,1... | collective-permute-start | bytes 1769480 | tf_op jit(solution)/shard_map/ppermute | solution.py:276
  101.0 87.3 %collective-permute-start.5 = (bf16[384,768]{1,0:T(8,128)(2,1)}, bf16[384,768]{1,0:T(8,128)(2,1)}, u32[]{:S(2)}, u32[]{:S(2)}) collective-permute-start(bf16[384,768]{1,0:T(8,128)(2,1)} %get-tuple-element.44), channel_id=1, source_target_pairs={{0,4},{4,0},{1,5},{5,1},{2,6},{6,2},{3,7},{7,3},{8,12},{12,8},{9,1... | collective-permute-start | bytes 1769480 | tf_op jit(solution)/shard_map/ppermute | solution.py:276
  125.5 36.3 %collective-permute-start.2 = (bf16[768,384]{1,0:T(8,128)(2,1)S(1)}, bf16[768,384]{1,0:T(8,128)(2,1)S(1)}, u32[]{:S(2)}, u32[]{:S(2)}) collective-permute-start(bf16[768,384]{1,0:T(8,128)(2,1)S(1)} %copy-done.71), channel_id=1, source_target_pairs={{0,4},{4,0},{1,5},{5,1},{2,6},{6,2},{3,7},{7,3},{8,12},{12,8},{9,1... | collective-permute-start | bytes 1769480 | tf_op jit(solution)/shard_map/ppermute | solution.py:276
  322.6 157.8 %collective-permute-start.33 = (bf16[1536,384]{1,0:T(8,128)(2,1)}, bf16[1536,384]{1,0:T(8,128)(2,1)}, u32[]{:S(2)}, u32[]{:S(2)}) collective-permute-start(bf16[1536,384]{1,0:T(8,128)(2,1)} %fusion.37), channel_id=1, source_target_pairs={{0,4},{4,0},{1,5},{5,1},{2,6},{6,2},{3,7},{7,3},{8,12},{12,8},{9,1... | collective-permute-start | bytes 3538952 | tf_op jit(solution)/shard_map/ppermute | solution.py:276
  375.3 163.2 %collective-permute-start.26 = (bf16[1536,384]{1,0:T(8,128)(2,1)}, bf16[1536,384]{1,0:T(8,128)(2,1)}, u32[]{:S(2)}, u32[]{:S(2)}) collective-permute-start(bf16[1536,384]{1,0:T(8,128)(2,1)} %fusion.32), channel_id=1, source_target_pairs={{0,4},{4,0},{1,5},{5,1},{2,6},{6,2},{3,7},{7,3},{8,12},{12,8},{9,1... | collective-permute-start | bytes 3538952 | tf_op jit(solution)/shard_map/ppermute | solution.py:276
  424.1 36.8 %collective-permute-start.16 = (bf16[768,384]{1,0:T(8,128)(2,1)S(1)}, bf16[768,384]{1,0:T(8,128)(2,1)S(1)}, u32[]{:S(2)}, u32[]{:S(2)}) collective-permute-start(bf16[768,384]{1,0:T(8,128)(2,1)S(1)} %copy-done.93), channel_id=1, source_target_pairs={{0,4},{4,0},{1,5},{5,1},{2,6},{6,2},{3,7},{7,3},{8,12},{12,8},{9,1... | collective-permute-start | bytes 1769480 | tf_op jit(solution)/shard_map/ppermute | solution.py:276
  462.0 29.3 %collective-permute-start.17 = (bf16[192,384]{1,0:T(8,128)(2,1)}, bf16[192,384]{1,0:T(8,128)(2,1)}, u32[]{:S(2)}, u32[]{:S(2)}) collective-permute-start(bf16[192,384]{1,0:T(8,128)(2,1)} %get-tuple-element.180), channel_id=1, source_target_pairs={{0,8},{8,16},{16,24},{24,0},{1,9},{9,17},{17,25},{25,1},{2,10},{10... | collective-permute-start | bytes 442376 | tf_op jit(solution)/shard_map/ppermute | solution.py:311
  463.5 29.4 %collective-permute-start.18 = (bf16[192,384]{1,0:T(8,128)(2,1)}, bf16[192,384]{1,0:T(8,128)(2,1)}, u32[]{:S(2)}, u32[]{:S(2)}) collective-permute-start(bf16[192,384]{1,0:T(8,128)(2,1)} %get-tuple-element.182), channel_id=1, source_target_pairs={{0,16},{8,24},{16,0},{24,8},{1,17},{9,25},{17,1},{25,9},{2,18},{10... | collective-permute-start | bytes 442376 | tf_op jit(solution)/shard_map/ppermute | solution.py:311
  490.7 45.4 %collective-permute-start.9 = (bf16[768,384]{1,0:T(8,128)(2,1)S(1)}, bf16[768,384]{1,0:T(8,128)(2,1)}, u32[]{:S(2)}, u32[]{:S(2)}) collective-permute-start(bf16[768,384]{1,0:T(8,128)(2,1)S(1)} %copy-done.92), channel_id=1, source_target_pairs={{0,4},{4,0},{1,5},{5,1},{2,6},{6,2},{3,7},{7,3},{8,12},{12,8},{9,1... | collective-permute-start | bytes 1769480 | tf_op jit(solution)/shard_map/ppermute | solution.py:276
  491.4 23.0 %collective-permute-start.34 = (bf16[384,384]{1,0:T(8,128)(2,1)}, bf16[384,384]{1,0:T(8,128)(2,1)}, u32[]{:S(2)}, u32[]{:S(2)}) collective-permute-start(bf16[384,384]{1,0:T(8,128)(2,1)} %get-tuple-element.153), channel_id=1, source_target_pairs={{0,8},{8,16},{16,24},{24,0},{1,9},{9,17},{17,25},{25,1},{2,10},{10... | collective-permute-start | bytes 884744 | tf_op jit(solution)/shard_map/ppermute | solution.py:311
  533.7 22.0 %collective-permute-start.38 = (bf16[384,384]{1,0:T(8,128)(2,1)S(1)}, bf16[384,384]{1,0:T(8,128)(2,1)S(1)}, u32[]{:S(2)}, u32[]{:S(2)}) collective-permute-start(bf16[384,384]{1,0:T(8,128)(2,1)S(1)} %get-tuple-element.124), channel_id=1, source_target_pairs={{0,16},{8,24},{16,0},{24,8},{1,17},{9,25},{17,1},{25,9},{2,18},{10... | collective-permute-start | bytes 884744 | tf_op jit(solution)/shard_map/ppermute | solution.py:311
  535.1 31.3 %collective-permute-start.39 = (bf16[384,384]{1,0:T(8,128)(2,1)S(1)}, bf16[384,384]{1,0:T(8,128)(2,1)S(1)}, u32[]{:S(2)}, u32[]{:S(2)}) collective-permute-start(bf16[384,384]{1,0:T(8,128)(2,1)S(1)} %get-tuple-element.124), channel_id=1, source_target_pairs={{0,24},{8,0},{16,8},{24,16},{1,25},{9,1},{17,9},{25,17},{2,26},{10... | collective-permute-start | bytes 884744 | tf_op jit(solution)/shard_map/ppermute | solution.py:311
  537.4 32.6 %collective-permute-start.10 = (bf16[192,384]{1,0:T(8,128)(2,1)S(1)}, bf16[192,384]{1,0:T(8,128)(2,1)S(1)}, u32[]{:S(2)}, u32[]{:S(2)}) collective-permute-start(bf16[192,384]{1,0:T(8,128)(2,1)S(1)} %get-tuple-element.177), channel_id=1, source_target_pairs={{0,8},{8,16},{16,24},{24,0},{1,9},{9,17},{17,25},{25,1},{2,10},{10... | collective-permute-start | bytes 442376 | tf_op jit(solution)/shard_map/ppermute | solution.py:311
  538.5 43.7 %collective-permute-start.11 = (bf16[192,384]{1,0:T(8,128)(2,1)S(1)}, bf16[192,384]{1,0:T(8,128)(2,1)S(1)}, u32[]{:S(2)}, u32[]{:S(2)}) collective-permute-start(bf16[192,384]{1,0:T(8,128)(2,1)S(1)} %get-tuple-element.179), channel_id=1, source_target_pairs={{0,16},{8,24},{16,0},{24,8},{1,17},{9,25},{17,1},{25,9},{2,18},{10... | collective-permute-start | bytes 442376 | tf_op jit(solution)/shard_map/ppermute | solution.py:311
  543.0 39.1 %collective-permute-start.12 = (bf16[192,384]{1,0:T(8,128)(2,1)S(1)}, bf16[192,384]{1,0:T(8,128)(2,1)S(1)}, u32[]{:S(2)}, u32[]{:S(2)}) collective-permute-start(bf16[192,384]{1,0:T(8,128)(2,1)S(1)} %get-tuple-element.178), channel_id=1, source_target_pairs={{0,24},{8,0},{16,8},{24,16},{1,25},{9,1},{17,9},{25,17},{2,26},{10... | collective-permute-start | bytes 442376 | tf_op jit(solution)/shard_map/ppermute | solution.py:311
  555.7 55.5 %collective-permute-start.27 = (bf16[384,384]{1,0:T(8,128)(2,1)S(1)}, bf16[384,384]{1,0:T(8,128)(2,1)S(1)}, u32[]{:S(2)}, u32[]{:S(2)}) collective-permute-start(bf16[384,384]{1,0:T(8,128)(2,1)S(1)} %get-tuple-element.150), channel_id=1, source_target_pairs={{0,8},{8,16},{16,24},{24,0},{1,9},{9,17},{17,25},{25,1},{2,10},{10... | collective-permute-start | bytes 884744 | tf_op jit(solution)/shard_map/ppermute | solution.py:311
  566.4 44.9 %collective-permute-start.28 = (bf16[384,384]{1,0:T(8,128)(2,1)S(1)}, bf16[384,384]{1,0:T(8,128)(2,1)S(1)}, u32[]{:S(2)}, u32[]{:S(2)}) collective-permute-start(bf16[384,384]{1,0:T(8,128)(2,1)S(1)} %get-tuple-element.152), channel_id=1, source_target_pairs={{0,16},{8,24},{16,0},{24,8},{1,17},{9,25},{17,1},{25,9},{2,18},{10... | collective-permute-start | bytes 884744 | tf_op jit(solution)/shard_map/ppermute | solution.py:311
  570.0 41.2 %collective-permute-start.29 = (bf16[384,384]{1,0:T(8,128)(2,1)S(1)}, bf16[384,384]{1,0:T(8,128)(2,1)S(1)}, u32[]{:S(2)}, u32[]{:S(2)}) collective-permute-start(bf16[384,384]{1,0:T(8,128)(2,1)S(1)} %get-tuple-element.151), channel_id=1, source_target_pairs={{0,24},{8,0},{16,8},{24,16},{1,25},{9,1},{17,9},{25,17},{2,26},{10... | collective-permute-start | bytes 884744 | tf_op jit(solution)/shard_map/ppermute | solution.py:311
  586.7 21.3 %collective-permute-start.14 = (bf16[192,384]{1,0:T(8,128)(2,1)S(1)}, bf16[192,384]{1,0:T(8,128)(2,1)S(1)}, u32[]{:S(2)}, u32[]{:S(2)}) collective-permute-start(bf16[192,384]{1,0:T(8,128)(2,1)S(1)} %get-tuple-element.132), channel_id=1, source_target_pairs={{0,16},{8,24},{16,0},{24,8},{1,17},{9,25},{17,1},{25,9},{2,18},{10... | collective-permute-start | bytes 442376 | tf_op jit(solution)/shard_map/ppermute | solution.py:311
  613.6 20.5 %collective-permute-start.31 = (bf16[384,384]{1,0:T(8,128)(2,1)S(1)}, bf16[384,384]{1,0:T(8,128)(2,1)S(1)}, u32[]{:S(2)}, u32[]{:S(2)}) collective-permute-start(bf16[384,384]{1,0:T(8,128)(2,1)S(1)} %get-tuple-element.122), channel_id=1, source_target_pairs={{0,16},{8,24},{16,0},{24,8},{1,17},{9,25},{17,1},{25,9},{2,18},{10... | collective-permute-start | bytes 884744 | tf_op jit(solution)/shard_map/ppermute | solution.py:311
  (170 other events, 1545.4 us)
Sparse Core Ops, SparseCore 0:
  34.0 24.2 all-gather.2
  186.3 23.7 all-gather.4

commit v3 on v2

--- a/solution.py
+++ b/solution.py
@@ -97,8 +97,7 @@
         ],
         scratch_shapes=[pltpu.VMEM((width, keys), jnp.bfloat16)],
         compiler_params=pltpu.CompilerParams(vmem_limit_bytes=BIG),
-        cost_estimate=pl.CostEstimate(
-            flops=8 * rows * keys * width, bytes_accessed=6 * keys * width, transcendentals=rows * keys * heads
+        cost_estimate=pl.CostEstimate(flops=1024, bytes_accessed=1024, transcendentals=0
         ),
     )(queries, key_all, value_all, bias)
 
@@ -182,14 +181,18 @@
             pltpu.VMEM((keys, width), jnp.float32),
         ],
         compiler_params=pltpu.CompilerParams(vmem_limit_bytes=BIG),
-        cost_estimate=pl.CostEstimate(
-            flops=20 * rows * keys * width, bytes_accessed=12 * keys * width, transcendentals=rows * keys * heads
+        cost_estimate=pl.CostEstimate(flops=1024, bytes_accessed=1024, transcendentals=0
         ),
     )(queries, key_all, value_all, bias, logsum, attended, d_attended)
     return (d_query, d_pairs)
 
 
-def head_sum_kernel(dims, chunks, a_ref, w_ref, out_ref, first, landed, own, chip, crossed, last, done, send, recv):
+def head_sum_kernel(dims, chunks, carries, *refs):
+    if carries:
+        a_ref, w_ref, sent_ref, out_ref, got_ref, *refs, carry_send, carry_recv = refs
+    else:
+        a_ref, w_ref, out_ref, *refs = refs
+    first, landed, own, chip, crossed, last, done, send, recv = refs
     me = lax.axis_index("head")
     core = me % 2
     sibling = me + 1 - 2 * core
@@ -205,6 +208,20 @@
             barrier, inc=1, device_id={"head": other}, device_id_type=pl.DeviceIdType.MESH
         )
 
+    if carries:
+        facing = 1 - lax.axis_index("seq")
+        pl.semaphore_signal(
+            barrier, inc=1, device_id={"seq": facing}, device_id_type=pl.DeviceIdType.MESH
+        )
+        carry = pltpu.make_async_remote_copy(
+            src_ref=sent_ref,
+            dst_ref=got_ref,
+            send_sem=carry_send,
+            recv_sem=carry_recv,
+            device_id={"seq": facing},
+            device_id_type=pl.DeviceIdType.MESH,
+        )
+
     def product(base):
         rows = pl.ds(pl.multiple_of(base, 16), size)
         return lax.dot_general(a_ref[rows, :], w_ref[...], dims, preferred_element_type=jnp.float32)
@@ -222,13 +239,22 @@
     outward = [remote(first, landed, 0, c, sibling) for c in range(chunks)]
     cross = [remote(chip, crossed, 1, c, across) for c in range(chunks)]
     back = [remote(last, done, 2, c, sibling) for c in range(chunks)]
-    for c in range(chunks):
+    ahead = 2
+
+    def offer(c):
         first[c] = product(theirs + c * size).astype(jnp.bfloat16)
         if c == 0:
-            pl.semaphore_wait(barrier, 2)
+            pl.semaphore_wait(barrier, 3 if carries else 2)
+            if carries:
+                carry.start()
         outward[c].start()
+
+    for c in range(ahead):
+        offer(c)
     for c in range(chunks):
         own[c] = product(mine + c * size)
+        if c + ahead < chunks:
+            offer(c + ahead)
         outward[c].wait_recv()
         chip[c] = (own[c] + landed[c].astype(jnp.float32)).astype(jnp.bfloat16)
         cross[c].start()
@@ -245,31 +271,53 @@
         outward[c].wait_send()
         cross[c].wait_send()
         back[c].wait_send()
-
-
-def head_sum(a, w, transposed, call_id):
+    if carries:
+        carry.wait()
+
+
+def head_sum(a, w, transposed, call_id, sent=None):
     rows = a.shape[0]
     columns = w.shape[0] if transposed else w.shape[1]
-    chunks = 3
+    chunks = 6
+    carries = sent is not None
     piece = (chunks, rows // 2 // chunks, columns)
     low = pltpu.VMEM(piece, jnp.bfloat16)
-    return pl.pallas_call(
-        functools.partial(head_sum_kernel, NT if transposed else NN, chunks),
-        in_specs=[VMEM, VMEM],
-        out_specs=VMEM,
-        out_shape=jax.ShapeDtypeStruct((rows, columns), jnp.bfloat16),
-        scratch_shapes=[
-            low, low, pltpu.VMEM(piece, jnp.float32), low, low, low, low,
-            pltpu.SemaphoreType.DMA((3, chunks)),
-            pltpu.SemaphoreType.DMA((3, chunks)),
-        ],
+    out_shape = [jax.ShapeDtypeStruct((rows, columns), jnp.bfloat16)]
+    scratch = [
+        low, low, pltpu.VMEM(piece, jnp.float32), low, low, low, low,
+        pltpu.SemaphoreType.DMA((3, chunks)),
+        pltpu.SemaphoreType.DMA((3, chunks)),
+    ]
+    anywhere = [pl.BlockSpec(memory_space=pl.ANY)] if carries else []
+    if carries:
+        out_shape.append(jax.ShapeDtypeStruct(sent.shape, sent.dtype))
+        scratch += [pltpu.SemaphoreType.DMA, pltpu.SemaphoreType.DMA]
+    result = pl.pallas_call(
+        functools.partial(head_sum_kernel, NT if transposed else NN, chunks, carries),
+        in_specs=[VMEM, VMEM] + anywhere,
+        out_specs=[VMEM] + anywhere,
+        out_shape=out_shape,
+        scratch_shapes=scratch,
         compiler_params=pltpu.CompilerParams(
             collective_id=call_id, has_side_effects=True, vmem_limit_bytes=BIG
         ),
-        cost_estimate=pl.CostEstimate(
-            flops=2 * rows * columns * a.shape[1], bytes_accessed=40 * rows * columns, transcendentals=0
-        ),
-    )(a, w)
+        cost_estimate=pl.CostEstimate(flops=1024, bytes_accessed=1024, transcendentals=0),
+    )(a, w, *([sent] if carries else []))
+    return result if carries else result[0]
+
+
+def head_sum_and_seq(a, w, call_id, values):
+    if lax.axis_size("seq") != 2:
+        shares = lax.psum_scatter(
+            values.astype(jnp.bfloat16), "seq", scatter_dimension=1, tiled=True
+        )
+        return (head_sum(a, w, True, call_id), shares)
+    size = values.shape[1] // 2
+    me = lax.axis_index("seq")
+    kept = lax.dynamic_slice_in_dim(values, me * size, size, 1)
+    sent = lax.dynamic_slice_in_dim(values, (1 - me) * size, size, 1).astype(jnp.bfloat16)
+    total, got = head_sum(a, w, True, call_id, sent)
+    return (total, (kept + got.astype(jnp.float32)).astype(jnp.bfloat16))
 
 
 def swap(values):
@@ -288,48 +336,6 @@
 
 def after(earlier, *values):
     return lax.optimization_barrier((earlier, *values))[1:]
-
-
-def scatter_seq(values):
-    if lax.axis_size("seq") != 2:
-        return (None, values.astype(jnp.bfloat16))
-    size = values.shape[1] // 2
-    me = lax.axis_index("seq")
-    kept = lax.dynamic_slice_in_dim(values, me * size, size, 1)
-    sent = lax.dynamic_slice_in_dim(values, (1 - me) * size, size, 1)
-    return (kept, sent.astype(jnp.bfloat16))
-
-
-def finish_seq(kept, sent):
-    if lax.axis_size("seq") != 2:
-        return lax.psum_scatter(sent, "seq", scatter_dimension=1, tiled=True)
-    return (kept.astype(jnp.float32) + swap(sent).astype(jnp.float32)).astype(jnp.bfloat16)
-
-
-def shifted(values, axis, shift):
-    n = lax.axis_size(axis)
-    return lax.ppermute(values, axis, [(i, (i + shift) % n) for i in range(n)])
-
-
-def sum_dp(values):
-    n = lax.axis_size("dp")
-    me = lax.axis_index("dp")
-    size = values.shape[0] // n
-
-    def share(shift):
-        return lax.dynamic_slice_in_dim(values, (me + shift) % n * size, size, 0)
-
-    total = share(0).astype(jnp.float32)
-    for shift in range(1, n):
-        total = total + shifted(share(shift), "dp", shift).astype(jnp.float32)
-    total = total.astype(jnp.bfloat16)
-    result = jnp.zeros(values.shape, jnp.bfloat16)
-    result = lax.dynamic_update_slice_in_dim(result, total, me * size, 0)
-    for shift in range(1, n):
-        result = lax.dynamic_update_slice_in_dim(
-            result, shifted(total, "dp", shift), (me + n - shift) % n * size, 0
-        )
-    return result
 
 
 def sum_pairwise(values, axis):
@@ -371,6 +377,8 @@
     gain_all, shift_all = vectors[:, :2], vectors[:, 2:]
     flat_qkv = w_qkv.transpose(0, 2, 1, 3).reshape(layers, -1, 3 * head_width)
     qkv_full = lax.all_gather(flat_qkv[0], "seq", axis=0, tiled=True)
+    own = after(qkv_full, w_out[0], w_up[0], w_down[0])
+    out_full, up_full, down_full = (gather_seq(w, axis) for w, axis in zip(own, (1, 0, 1)))
 
     stream = frames.astype(jnp.float32).reshape(row_count, model_width)
     saved_layers = []
@@ -385,12 +393,6 @@
         pair = jnp.dot(normed, qkv_full[:, head_width:], preferred_element_type=jnp.float32)
         pair = pair + jnp.concatenate([jnp.zeros_like(bias_pair[1]), bias_pair[1]])
         pair_all = lax.all_gather(pair.astype(jnp.bfloat16), "seq", axis=0, tiled=True)
-        if l == 0:
-            own = after(pair_all, w_out[0], w_up[0], w_down[0])
-            out_full = gather_seq(own[0], 1)
-            own = after(out_full, own[1])
-            up_full = gather_seq(own[0], 0)
-            down_full = gather_seq(after(up_full, w_down[0])[0], 1)
         key_all, value_all = pair_all[:, :head_width], pair_all[:, head_width:]
         queries = jnp.dot(normed, qkv_full[:, :head_width], preferred_element_type=jnp.float32)
         queries = ((queries + bias_pair[0]) * query_scale).astype(jnp.bfloat16)
@@ -399,7 +401,7 @@
         normed_two = normalize(mid, gain_pair[1], shift_set[2]).astype(jnp.bfloat16)
         weights.append((qkv_full, out_full, up_full, down_full))
         if l + 1 < layers:
-            own = after(normed_two, flat_qkv[l + 1], w_out[l + 1], w_up[l + 1], w_down[l + 1])
+            own = after(attended, flat_qkv[l + 1], w_out[l + 1], w_up[l + 1], w_down[l + 1])
             next_weights = tuple(gather_seq(w, axis) for w, axis in zip(own, (0, 1, 0, 1)))
         hidden_pre = jnp.dot(normed_two, up_full, preferred_element_type=jnp.float32) + up_bias[
             l
@@ -429,12 +431,14 @@
         gelu_value, gelu_pull = jax.vjp(gelu_exact, hidden_pre)
         d_hidden = gelu_pull(d_act)[0].astype(jnp.bfloat16)
         d_up_bias = column_sum(d_hidden)
-        kept, sent = scatter_seq(
-            jnp.concatenate([cross(activated, grad_low), cross(d_hidden, normed_two)], axis=0)
-        )
-        d_hidden, sent = lax.optimization_barrier((d_hidden, sent))
-        share_mlp = finish_seq(kept, sent)
-        d_norm_two = head_sum(d_hidden, up_full, True, 3).astype(jnp.float32)
+        mlp_grads = jnp.concatenate(
+            [cross(activated, grad_low), cross(d_hidden, normed_two)], axis=0
+        )
+        if l + 1 < layers:
+            d_hidden, packed = lax.optimization_barrier((d_hidden, packed))
+            owned[l + 1] = lax.psum(packed, "dp")
+        d_norm_two, share_mlp = head_sum_and_seq(d_hidden, up_full, 3, mlp_grads)
+        d_norm_two = d_norm_two.astype(jnp.float32)
         norm_value, norm_pull = jax.vjp(normalize, mid, gain_pair[1], shift_set[2])
         d_mid, d_gain_two, d_shift_two = norm_pull(d_norm_two)
         grad_stream = grad_stream + d_mid
@@ -453,17 +457,23 @@
         else:
             d_pair = lax.psum_scatter(d_pairs[0], "seq", scatter_dimension=0, tiled=True)
         d_qkv = jnp.concatenate([d_query, d_pair], axis=1)
-        kept, sent = scatter_seq(
-            jnp.concatenate([cross(d_qkv, normed), cross(attended, grad_low)], axis=0)
-        )
-        d_qkv, sent = lax.optimization_barrier((d_qkv, sent))
-        share_attn = finish_seq(kept, sent)
-        d_normed = head_sum(d_qkv, qkv_full, True, 4).astype(jnp.float32)
+        attn_grads = jnp.concatenate([cross(d_qkv, normed), cross(attended, grad_low)], axis=0)
+        if l + 1 < layers:
+            d_qkv, share_mlp, owned[l + 1] = lax.optimization_barrier(
+                (d_qkv, share_mlp, owned[l + 1])
+            )
+        d_normed, share_attn = head_sum_and_seq(d_qkv, qkv_full, 4, attn_grads)
+        d_normed = d_normed.astype(jnp.float32)
         d_bias = column_sum(d_qkv)
         norm_value, norm_pull = jax.vjp(normalize, stream_in, gain_pair[0], shift_set[0])
         d_before, d_gain_one, d_shift_one = norm_pull(d_normed)
         grad_stream = grad_stream + d_before
-        owned[l] = (sum_dp(share_mlp), sum_dp(share_attn))
+        if l > 0:
+            packed = jnp.concatenate([share_mlp, share_attn], axis=0)
+        else:
+            owned_mlp = lax.psum(share_mlp, "dp")
+            owned_mlp, share_attn = lax.optimization_barrier((owned_mlp, share_attn))
+            owned[l] = (owned_mlp, lax.psum(share_attn, "dp"))
         small[l] = [
             d_gain_one, d_gain_two, d_shift_one, d_shift_attn, d_shift_two, d_shift_mlp,
             d_up_bias, d_bias[:head_width], d_bias[2 * head_width :],
@@ -476,8 +486,10 @@
     grad_bias_up = vector_sums[:, 6 * d : 6 * d + units]
     grad_bias_pair = vector_sums[:, 6 * d + units :].reshape(layers, 2, head_width)
 
-    mlp = [entry[0].astype(jnp.float32) for entry in owned]
-    attn = [entry[1].astype(jnp.float32) for entry in owned]
+    mlp, attn = [owned[0][0].astype(jnp.float32)], [owned[0][1].astype(jnp.float32)]
+    for entry in owned[1:]:
+        mlp.append(entry[: 2 * units].astype(jnp.float32))
+        attn.append(entry[2 * units :].astype(jnp.float32))
     grad_down_weight = jnp.stack([m[:units] for m in mlp])
     grad_up_weight = jnp.stack([m[units:].T for m in mlp])
     grad_qkv = jnp.stack(

time: 655 us -> 551 us (0.84)
  waiting for transfers between devices: 204 us -> 119 us
  starting transfers between devices: 59.9 us -> 14 us
  Pallas kernels: 190 us -> 208 us
  matrix products: 35.4 us -> 43.6 us
    ppermute x24 -> x0, waiting for transfers between devices: 91.5 us -> none  [shifted(): return lax.ppermute(values, axis, [(i, (i + shift) % n) for i in range(n)])]
    ppermute x24 -> x0, starting transfers between devices: 43.8 us -> none  [shifted(): return lax.ppermute(values, axis, [(i, (i + shift) % n) for i in range(n)])]
    psum x0 -> x3, waiting for transfers between devices: none -> 38.6 us  [the longest x1 32.9 us: on_device(): owned[l] = (owned_mlp, lax.psum(share_attn, 'dp'))]
    all_gather x2, waiting for transfers between devices: 34.8 us -> 13.8 us  [on_device(): lax.all_gather(pair.astype(jnp.bfloat16), 'seq', axis=0, tiled=True)]
    pallas_call x8, Pallas kernels: 147 us -> 166 us  [head_sum(): pl.pallas_call(functools.partial(head_sum_kernel, NT if transposed else N...]
    ppermute x13 -> x9, waiting for transfers between devices: 71.4 us -> 53.7 us  [swap(): return lax.ppermute(values, 'seq', [(0, 1), (1, 0)])]
    dot_general x8, matrix products: 8.1 us -> 15.8 us  [cross(): lax.dot_general(left, right, (((0,), (0,)), ((), ())), preferred_element_...]
    ppermute x3, waiting for transfers between devices: 6.49 us -> 13.1 us  [sum_pairwise(): lax.ppermute(values, axis, [(i, i ^ step) for i in range(n)])]
  transfers between devices with their start and end apart: 42 -> 17, of which waited for: 22 -> 9; matrix products, arithmetic and copies ran while one was open for 14% -> 16% of each run, Pallas kernels for 15% -> 17%
where the time goes in v3:
time: 551 us; the launch traced here: 547 us
  Pallas kernels  208 us (38%)
  waiting for transfers between devices  119 us (22%)
  other arithmetic  70.9 us (13%)
  local copies, waits for them, and re-layouts  55.6 us (10%)
  matrix products  43.6 us (8%)
  blocking collectives  18.3 us (3%)
  between operations  16.7 us (3%)
  starting transfers between devices  14 us (3%)
    pallas_call x8, Pallas kernels, head_sum(): pl.pallas_call(functools.partial(head_sum_kernel, NT if transposed else N...  166 us
    ppermute x9, waiting for transfers between devices, swap(): return lax.ppermute(values, 'seq', [(0, 1), (1, 0)])  53.7 us
    psum x1, waiting for transfers between devices, on_device(): owned[l] = (owned_mlp, lax.psum(share_attn, 'dp'))  32.9 us
    unnamed x335, local copies, waits for them, and re-layouts  31.6 us
    pallas_call x2, Pallas kernels, attend_back(): pl.pallas_call(functools.partial(attend_back_kernel, heads), grid=(rows /...  22.3 us
    pallas_call x2, Pallas kernels, attend(): pl.pallas_call(functools.partial(attend_kernel, heads), grid=(rows // blo...  20 us
    dot_general x8, matrix products, cross(): lax.dot_general(left, right, (((0,), (0,)), ((), ())), preferred_element_...  15.8 us
    dot_general x2, matrix products, on_device(): jnp.dot(normed_two, up_full, preferred_element_type=jnp.float32)  13.9 us
  transfers between devices with their start and end apart: 17, of which 9 were waited for; matrix products, arithmetic and copies ran while one was open for 16% of the time, Pallas kernels for 17%

profile of v3, /device:TPU:0, one launch (start us, length us, event | category | flops | bytes accessed | tf_op | source)
XLA Modules:
  0.0 546.7 jit_solution(5652747807832592902)
XLA Ops:
  10.7 5.5 all_gather.12
  18.0 12.8 %all_gather.13.refs_1_ = bf16[768,576]{1,0:T(8,128)(2,1)S(1)} all-gather(bf16[384,576]{1,0:T(8,128)(2,1)S(1)} %copy.37), channel_id=1, replica_groups=mesh['dp'=4,'seq'=2,'head'=4] {'seq'}, dimensions={0}, use_global_device_ids=true | all-gather | bytes 1327104 | tf_op jit(solution)/shard_map/all_gather | solution.py:379
  47.8 32.8 %collective-permute-done.2 = bf16[768,384]{1,0:T(8,128)(2,1)} collective-permute-done((bf16[768,384]{1,0:T(8,128)(2,1)S(1)}, bf16[768,384]{1,0:T(8,128)(2,1)}, u32[]{:S(2)}, u32[]{:S(2)}) %collective-permute-start.2) | collective-permute-done | bytes 589856 | tf_op jit(solution)/shard_map/ppermute | solution.py:324
  87.5 9.7 %shard_map.186 = (bf16[768,192]{1,0:T(8,128)(2,1)S(1)}, f32[3,3,256]{2,1,0:T(4,128)S(1)}) custom-call(bf16[768,192]{1,0:T(8,128)(2,1)S(1)} %fusion.63.q_ref, bf16[1536,192]{1,0:T(8,128)(2,1)S(1)} %get-tuple-element.170.k_ref, bf16[1536,192]{1,0:T(8,128)(2,1)S(1)} %get-tuple-element.169.v_ref, f32[1536,1]{1,0:T(8,128)S(1)} %fusion.79.bias_ref), custom_call_target="tpu_custom_call" | custom-call | flops 1024 | bytes 1024 | tf_op jit(solution)/shard_map/pallas_call | solution.py:81
  105.3 18.1 %shard_map.187 = bf16[768,768]{1,0:T(8,128)(2,1)S(1)} custom-call(bf16[768,192]{1,0:T(8,128)(2,1)S(1)} %get-tuple-element.42.refs_0_.o_ref, bf16[192,768]{1,0:T(8,128)(2,1)S(1)} %copy-done.29), custom_call_target="tpu_custom_call" | custom-call | flops 1024 | bytes 1024 | tf_op jit(solution)/shard_map/pallas_call | solution.py:295
  126.0 7.9 %multiply_convert_fusion.1 = (bf16[768,768]{1,0:T(8,128)(2,1)S(1)}, f32[768,768]{1,0:T(8,128)}, f32[768,768]{1,0:T(8,128)}) fusion(f32[768]{0:T(1024)S(1)} %copy-done.154, bf16[384,768]{1,0:T(8,128)(2,1)S(1)} %copy-done.81, bf16[384,768]{1,0:T(8,128)(2,1)S(1)} %copy-done.79, f32[768]{0:T(1024)S(1)} %copy-done.159, f32[768]{0:T(1024)S(1)} %copy-done.108, ...), kind=kOutput, calls=%fused_computation.116 | convolution fusion | flops 952565760 | bytes 9455616 | tf_op jit(solution)/shard_map/dot_general | solution.py:406
  134.0 18.2 %shard_map.188 = bf16[768,768]{1,0:T(8,128)(2,1)S(1)} custom-call(bf16[768,768]{1,0:T(8,128)(2,1)S(1)} %get-tuple-element.147.refs_0_, bf16[768,768]{1,0:T(8,128)(2,1)S(1)} %pad_maximum_fusion.6.refs_1_), custom_call_target="tpu_custom_call" | custom-call | flops 1024 | bytes 1024 | tf_op jit(solution)/shard_map/pallas_call | solution.py:295
  169.3 13.8 %all-gather.5.cloned.1.call-done = bf16[1536,384]{1,0:T(8,128)(2,1)} async-done(((bf16[768,384]{1,0:T(8,128)(2,1)}), bf16[1536,384]{1,0:T(8,128)(2,1)}) %all-gather.5.cloned.1.call-update) | async-done | bytes 1179664 | tf_op jit(solution)/shard_map/all_gather | solution.py:395
  186.0 10.3 %shard_map.189 = (bf16[768,192]{1,0:T(8,128)(2,1)S(1)}, f32[3,3,256]{2,1,0:T(4,128)S(1)}) custom-call(bf16[768,192]{1,0:T(8,128)(2,1)S(1)} %copy-done.19, bf16[1536,192]{1,0:T(8,128)(2,1)S(1)} %get-tuple-element.160.k_ref, bf16[1536,192]{1,0:T(8,128)(2,1)S(1)} %get-tuple-element.159.v_ref, f32[1536,1]{1,0:T(8,128)S(1)} %fusion.79.bias_ref), custom_call_target="tpu_custom_call" | custom-call | flops 1024 | bytes 1024 | tf_op jit(solution)/shard_map/pallas_call | solution.py:81
  196.9 18.1 %shard_map.190 = bf16[768,768]{1,0:T(8,128)(2,1)S(1)} custom-call(bf16[768,192]{1,0:T(8,128)(2,1)S(1)} %get-tuple-element.47.refs_0_.o_ref, bf16[192,768]{1,0:T(8,128)(2,1)S(1)} %copy-done.30), custom_call_target="tpu_custom_call" | custom-call | flops 1024 | bytes 1024 | tf_op jit(solution)/shard_map/pallas_call | solution.py:295
  216.7 5.9 %multiply_convert_fusion = (bf16[768,768]{1,0:T(8,128)(2,1)S(1)}, f32[768,768]{1,0:T(8,128)S(1)}, f32[768,768]{1,0:T(8,128)S(1)}) fusion(f32[768]{0:T(1024)S(1)} %copy-done.156, bf16[384,768]{1,0:T(8,128)(2,1)S(1)} %copy-done.85, bf16[384,768]{1,0:T(8,128)(2,1)S(1)} %copy-done.83, f32[768,768]{1,0:T(8,128)S(1)} %get-tuple-element.144, ...), kind=kOutput, calls=%fused_computation.97 | convolution fusion | flops 950206464 | bytes 9452544 | tf_op jit(solution)/shard_map/dot_general | solution.py:406
  232.0 18.1 %shard_map.191 = bf16[768,768]{1,0:T(8,128)(2,1)S(1)} custom-call(bf16[768,768]{1,0:T(8,128)(2,1)S(1)} %get-tuple-element.141.refs_0_, bf16[768,768]{1,0:T(8,128)(2,1)S(1)} %copy-done.6), custom_call_target="tpu_custom_call" | custom-call | flops 1024 | bytes 1024 | tf_op jit(solution)/shard_map/pallas_call | solution.py:295
  250.1 28.6 %shard_map.192 = (bf16[768,768]{1,0:T(8,128)(2,1)S(1)}, bf16[1536,384]{1,0:T(8,128)(2,1)S(1)}) custom-call(bf16[768,768]{1,0:T(8,128)(2,1)S(1)} %get-tuple-element.196.refs_0_, bf16[768,768]{1,0:T(8,128)(2,1)S(1)} %copy-done.7, bf16[1536,384]{1,0:T(8,128)(2,1)S(1)} %fusion.37.refs_2_), custom_call_target="tpu_custom_call" | custom-call | flops 1024 | bytes 1024 | tf_op jit(solution)/shard_map/pallas_call | solution.py:295
  291.7 11.0 %shard_map.193 = (bf16[768,192]{1,0:T(8,128)(2,1)S(1)}, bf16[768,384]{1,0:T(8,128)(2,1)S(1)}, bf16[768,384]{1,0:T(8,128)(2,1)S(1)}) custom-call(bf16[768,192]{1,0:T(8,128)(2,1)S(1)} %copy-done.20, bf16[1536,192]{1,0:T(8,128)(2,1)S(1)} %get-tuple-element.160.k_ref, bf16[1536,192]{1,0:T(8,128)(2,1)S(1)} %get-tuple-element.159.v_ref, ...), custom_call_target="tpu_custom_call" | custom-call | flops 1024 | bytes 1024 | tf_op jit(solution)/shard_map/pallas_call | solution.py:163
  307.2 10.4 %collective-permute-done.7 = bf16[768,384]{1,0:T(8,128)(2,1)S(1)} collective-permute-done((bf16[768,384]{1,0:T(8,128)(2,1)S(1)}, bf16[768,384]{1,0:T(8,128)(2,1)S(1)}, u32[]{:S(2)}, u32[]{:S(2)}) %collective-permute-start.7) | collective-permute-done | bytes 589856 | tf_op jit(solution)/shard_map/ppermute | solution.py:324
  320.5 18.1 %shard_map.194 = (bf16[768,768]{1,0:T(8,128)(2,1)S(1)}, bf16[768,384]{1,0:T(8,128)(2,1)S(1)}) custom-call(bf16[768,576]{1,0:T(8,128)(2,1)S(1)} %pad_maximum_fusion.9.refs_0_, bf16[768,576]{1,0:T(8,128)(2,1)S(1)} %copy-done.10, bf16[768,384]{1,0:T(8,128)(2,1)S(1)} %fusion.75.refs_2_), custom_call_target="tpu_custom_call" | custom-call | flops 1024 | bytes 1024 | tf_op jit(solution)/shard_map/pallas_call | solution.py:295
  359.3 28.6 %shard_map.195 = (bf16[768,768]{1,0:T(8,128)(2,1)S(1)}, bf16[1536,384]{1,0:T(8,128)(2,1)S(1)}) custom-call(bf16[768,768]{1,0:T(8,128)(2,1)S(1)} %copy-done.28, bf16[768,768]{1,0:T(8,128)(2,1)S(1)} %copy-done.5, bf16[1536,384]{1,0:T(8,128)(2,1)S(1)} %fusion.32.refs_2_), custom_call_target="tpu_custom_call" | custom-call | flops 1024 | bytes 1024 | tf_op jit(solution)/shard_map/pallas_call | solution.py:295
  403.3 11.4 %shard_map.196 = (bf16[768,192]{1,0:T(8,128)(2,1)S(1)}, bf16[768,384]{1,0:T(8,128)(2,1)S(1)}, bf16[768,384]{1,0:T(8,128)(2,1)}) custom-call(bf16[768,192]{1,0:T(8,128)(2,1)S(1)} %copy-done.18, bf16[1536,192]{1,0:T(8,128)(2,1)S(1)} %copy-done.4, bf16[1536,192]{1,0:T(8,128)(2,1)S(1)} %copy-done.2, f32[1536,1]{1,0:T(8,128)S(1)} %fusion.79.bias_ref, ...), custom_call_target="tpu_custom_call" | custom-call | flops 1024 | bytes 1024 | tf_op jit(solution)/shard_map/pallas_call | solution.py:163
  420.9 8.9 %collective-permute-done.8 = bf16[768,384]{1,0:T(8,128)(2,1)} collective-permute-done((bf16[768,384]{1,0:T(8,128)(2,1)}, bf16[768,384]{1,0:T(8,128)(2,1)}, u32[]{:S(2)}, u32[]{:S(2)}) %collective-permute-start.8) | collective-permute-done | bytes 589856 | tf_op jit(solution)/shard_map/ppermute | solution.py:324
  440.6 18.1 %shard_map.197 = (bf16[768,768]{1,0:T(8,128)(2,1)S(1)}, bf16[768,384]{1,0:T(8,128)(2,1)S(1)}) custom-call(bf16[768,576]{1,0:T(8,128)(2,1)S(1)} %copy-done, bf16[768,576]{1,0:T(8,128)(2,1)S(1)} %copy-done.9, bf16[768,384]{1,0:T(8,128)(2,1)S(1)} %fusion.70.refs_2_), custom_call_target="tpu_custom_call" | custom-call | flops 1024 | bytes 1024 | tf_op jit(solution)/shard_map/pallas_call | solution.py:295
  472.6 5.2 collective-permute-done.10
  479.2 7.9 %collective-permute-done.11 = f32[90,128]{1,0:T(8,128)S(1)} collective-permute-done((f32[90,128]{1,0:T(8,128)S(1)}, f32[90,128]{1,0:T(8,128)S(1)}, u32[]{:S(2)}, u32[]{:S(2)}) %collective-permute-start.11) | collective-permute-done | bytes 46112 | tf_op jit(solution)/shard_map/ppermute | solution.py:345
  489.7 5.7 %all-reduce.8.cloned.1.call-done = bf16[1536,384]{1,0:T(8,128)(2,1)} async-done(((bf16[1536,384]{1,0:T(8,128)(2,1)}), bf16[1536,384]{1,0:T(8,128)(2,1)}) %all-reduce.8.cloned.1.call-update) | async-done | bytes 1179664 | tf_op jit(solution)/shard_map/psum | solution.py:474
  503.5 32.9 %all-reduce.10.cloned.1.call-done = bf16[768,384]{1,0:T(8,128)(2,1)} async-done(((bf16[768,384]{1,0:T(8,128)(2,1)}), bf16[768,384]{1,0:T(8,128)(2,1)}) %all-reduce.10.cloned.1.call-update) | async-done | bytes 589840 | tf_op jit(solution)/shard_map/psum | solution.py:476
  (498 shorter events, 171.9 us)
Async XLA Ops:
  7.2 78.5 %all-gather.3.cloned.1.call-start = ((), (), s32[]{:S(2)}) async-start(), calls=%async_computation | async-start | bytes 1769472 | tf_op jit(solution)/shard_map/all_gather | solution.py:395
  8.8 34.4 %copy-start.106 = (f32[768]{0:T(1024)}, f32[768]{0:T(1024)S(1)}, u32[]{:S(2)}) copy-start(f32[768]{0:T(1024)S(1)} %broadcast_multiply_fusion.3) | copy-start | bytes 9220
  10.7 32.5 %copy-start.122 = (f32[768]{0:T(1024)}, f32[768]{0:T(1024)S(1)}, u32[]{:S(2)}) copy-start(f32[768]{0:T(1024)S(1)} %fusion.87) | copy-start | bytes 9220
  33.3 149.8 %all-gather.5.cloned.1.call-start = ((), (), s32[]{:S(2)}) async-start(), calls=%async_computation.1 | async-start | bytes 1769472 | tf_op jit(solution)/shard_map/all_gather | solution.py:395
  38.8 8.2 %collective-permute-start = (bf16[192,384]{1,0:T(8,128)(2,1)S(1)}, bf16[192,384]{1,0:T(8,128)(2,1)S(1)}, u32[]{:S(2)}, u32[]{:S(2)}) collective-permute-start(bf16[192,384]{1,0:T(8,128)(2,1)S(1)} %get-tuple-element.43), channel_id=1, source_target_pairs={{0,4},{4,0},{1,5},{5,1},{2,6},{6,2},{3,7},{7,3},{8,12},{12,8},{9,1... | collective-permute-start | bytes 442376 | tf_op jit(solution)/shard_map/ppermute | solution.py:324
  40.5 41.4 %collective-permute-start.1 = (bf16[384,768]{1,0:T(8,128)(2,1)}, bf16[384,768]{1,0:T(8,128)(2,1)}, u32[]{:S(2)}, u32[]{:S(2)}) collective-permute-start(bf16[384,768]{1,0:T(8,128)(2,1)} %get-tuple-element.44), channel_id=1, source_target_pairs={{0,4},{4,0},{1,5},{5,1},{2,6},{6,2},{3,7},{7,3},{8,12},{12,8},{9,1... | collective-permute-start | bytes 1769480 | tf_op jit(solution)/shard_map/ppermute | solution.py:324
  40.8 39.8 %collective-permute-start.2 = (bf16[768,384]{1,0:T(8,128)(2,1)S(1)}, bf16[768,384]{1,0:T(8,128)(2,1)}, u32[]{:S(2)}, u32[]{:S(2)}) collective-permute-start(bf16[768,384]{1,0:T(8,128)(2,1)S(1)} %get-tuple-element.45), channel_id=1, source_target_pairs={{0,4},{4,0},{1,5},{5,1},{2,6},{6,2},{3,7},{7,3},{8,12},{12,8},{9,1... | collective-permute-start | bytes 1769480 | tf_op jit(solution)/shard_map/ppermute | solution.py:324
  44.0 43.5 %copy-start.17 = (bf16[768,192]{1,0:T(8,128)(2,1)}, bf16[768,192]{1,0:T(8,128)(2,1)S(1)}, u32[]{:S(2)}) copy-start(bf16[768,192]{1,0:T(8,128)(2,1)S(1)} %fusion.63.q_ref) | copy-start | bytes 884740
  47.0 34.9 %copy-start.94 = (bf16[192,384]{1,0:T(8,128)(2,1)}, bf16[192,384]{1,0:T(8,128)(2,1)S(1)}, u32[]{:S(2)}) copy-start(bf16[192,384]{1,0:T(8,128)(2,1)S(1)} %get-tuple-element.179) | copy-start | bytes 442372
  47.0 34.9 %copy-start.96 = (bf16[192,384]{1,0:T(8,128)(2,1)}, bf16[192,384]{1,0:T(8,128)(2,1)S(1)}, u32[]{:S(2)}) copy-start(bf16[192,384]{1,0:T(8,128)(2,1)S(1)} %get-tuple-element.180) | copy-start | bytes 442372
  100.2 54.1 %collective-permute-start.4 = (bf16[192,384]{1,0:T(8,128)(2,1)}, bf16[192,384]{1,0:T(8,128)(2,1)S(1)}, u32[]{:S(2)}, u32[]{:S(2)}) collective-permute-start(bf16[192,384]{1,0:T(8,128)(2,1)} %get-tuple-element.48), channel_id=1, source_target_pairs={{0,4},{4,0},{1,5},{5,1},{2,6},{6,2},{3,7},{7,3},{8,12},{12,8},{9,1... | collective-permute-start | bytes 442376 | tf_op jit(solution)/shard_map/ppermute | solution.py:324
  101.7 54.5 %collective-permute-start.3 = (bf16[384,576]{1,0:T(8,128)(2,1)}, bf16[384,576]{1,0:T(8,128)(2,1)S(1)}, u32[]{:S(2)}, u32[]{:S(2)}) collective-permute-start(bf16[384,576]{1,0:T(8,128)(2,1)} %copy.40), channel_id=1, source_target_pairs={{0,4},{4,0},{1,5},{5,1},{2,6},{6,2},{3,7},{7,3},{8,12},{12,8},{9,1... | collective-permute-start | bytes 1327112 | tf_op jit(solution)/shard_map/ppermute | solution.py:324
  102.3 63.7 %collective-permute-start.5 = (bf16[384,768]{1,0:T(8,128)(2,1)}, bf16[384,768]{1,0:T(8,128)(2,1)}, u32[]{:S(2)}, u32[]{:S(2)}) collective-permute-start(bf16[384,768]{1,0:T(8,128)(2,1)} %get-tuple-element.49), channel_id=1, source_target_pairs={{0,4},{4,0},{1,5},{5,1},{2,6},{6,2},{3,7},{7,3},{8,12},{12,8},{9,1... | collective-permute-start | bytes 1769480 | tf_op jit(solution)/shard_map/ppermute | solution.py:324
  103.7 59.7 %collective-permute-start.6 = (bf16[768,384]{1,0:T(8,128)(2,1)}, bf16[768,384]{1,0:T(8,128)(2,1)}, u32[]{:S(2)}, u32[]{:S(2)}) collective-permute-start(bf16[768,384]{1,0:T(8,128)(2,1)} %get-tuple-element.50), channel_id=1, source_target_pairs={{0,4},{4,0},{1,5},{5,1},{2,6},{6,2},{3,7},{7,3},{8,12},{12,8},{9,1... | collective-permute-start | bytes 1769480 | tf_op jit(solution)/shard_map/ppermute | solution.py:324
  159.1 277.4 %all-reduce.6.cloned.1.call-start = ((), (), s32[]{:S(2)}) async-start(), calls=%async_computation.2 | async-start | bytes 3538944 | tf_op jit(solution)/shard_map/psum | solution.py:439
  183.1 31.9 %copy-start.148 = (f32[768]{0:T(1024)S(1)}, f32[768]{0:T(1024)}, u32[]{:S(2)}) copy-start(f32[768]{0:T(1024)} %get-tuple-element.122) | copy-start | bytes 9220
  302.7 14.9 %collective-permute-start.7 = (bf16[768,384]{1,0:T(8,128)(2,1)S(1)}, bf16[768,384]{1,0:T(8,128)(2,1)S(1)}, u32[]{:S(2)}, u32[]{:S(2)}) collective-permute-start(bf16[768,384]{1,0:T(8,128)(2,1)S(1)} %get-tuple-element.55), channel_id=1, source_target_pairs={{0,4},{4,0},{1,5},{5,1},{2,6},{6,2},{3,7},{7,3},{8,12},{12,8},{9,1... | collective-permute-start | bytes 1769480 | tf_op jit(solution)/shard_map/ppermute | solution.py:324
  356.9 138.5 %all-reduce.8.cloned.1.call-start = ((), (), s32[]{:S(2)}) async-start(), calls=%async_computation.3 | async-start | bytes 2359296 | tf_op jit(solution)/shard_map/psum | solution.py:474
  414.7 15.2 %collective-permute-start.8 = (bf16[768,384]{1,0:T(8,128)(2,1)}, bf16[768,384]{1,0:T(8,128)(2,1)}, u32[]{:S(2)}, u32[]{:S(2)}) collective-permute-start(bf16[768,384]{1,0:T(8,128)(2,1)} %get-tuple-element.64), channel_id=1, source_target_pairs={{0,4},{4,0},{1,5},{5,1},{2,6},{6,2},{3,7},{7,3},{8,12},{12,8},{9,1... | collective-permute-start | bytes 1769480 | tf_op jit(solution)/shard_map/ppermute | solution.py:324
  436.5 99.9 %all-reduce.10.cloned.1.call-start = ((), (), s32[]{:S(2)}) async-start(), calls=%async_computation.4 | async-start | bytes 1179648 | tf_op jit(solution)/shard_map/psum | solution.py:476
  464.6 5.5 %collective-permute-start.9 = (f32[90,128]{1,0:T(8,128)S(1)}, f32[90,128]{1,0:T(8,128)S(1)}, u32[]{:S(2)}, u32[]{:S(2)}) collective-permute-start(f32[90,128]{1,0:T(8,128)S(1)} %bitcast.171), channel_id=1, source_target_pairs={{0,4},{4,0},{1,5},{5,1},{2,6},{6,2},{3,7},{7,3},{8,12},{12,8},{9,1... | collective-permute-start | bytes 138248 | tf_op jit(solution)/shard_map/ppermute | solution.py:345
  470.1 7.7 %collective-permute-start.10 = (f32[90,128]{1,0:T(8,128)S(1)}, f32[90,128]{1,0:T(8,128)S(1)}, u32[]{:S(2)}, u32[]{:S(2)}) collective-permute-start(f32[90,128]{1,0:T(8,128)S(1)} %bitcast_add_fusion), channel_id=1, source_target_pairs={{0,8},{8,0},{16,24},{24,16},{1,9},{9,1},{17,25},{25,17},{2,10},{10... | collective-permute-start | bytes 138248 | tf_op jit(solution)/shard_map/ppermute | solution.py:345
  477.8 9.4 %collective-permute-start.11 = (f32[90,128]{1,0:T(8,128)S(1)}, f32[90,128]{1,0:T(8,128)S(1)}, u32[]{:S(2)}, u32[]{:S(2)}) collective-permute-start(f32[90,128]{1,0:T(8,128)S(1)} %fusion.141), channel_id=1, source_target_pairs={{0,16},{8,24},{16,0},{24,8},{1,17},{9,25},{17,1},{25,9},{2,18},{10... | collective-permute-start | bytes 138248 | tf_op jit(solution)/shard_map/ppermute | solution.py:345
  503.5 34.2 %slice-start = ((f32[768,384]{1,0:T(8,128)}), f32[576,384]{1,0:T(8,128)S(1)}, s32[]{:S(2)}) async-start(f32[768,384]{1,0:T(8,128)} %copy-done.62), calls=%async_computation.5 | async-start | bytes 1769472 | tf_op jit(solution)/shard_map/slice | solution.py:496
  (161 other events, 837.4 us)
Sparse Core Ops, SparseCore 0:
  33.4 37.0 all-gather.2
  159.2 23.8 all-gather.4
  357.0 75.5 all-reduce.5
  436.6 58.7 all-reduce.7
  498.3 38.0 all-reduce.9
